TPU v7x, 32 devices: a whole 2x2x4 slice. The times are simulated.
32 devices in a mesh: tile: 8 (over y, x, core), trc: 4 (over z).
Axes of the slice: x: 2, y: 2, z: 4, core: 2. Of those that a mesh axis runs over, the one named last changes fastest.
Arguments:
- tracers: float32 [16, 8, 64, 128], P('trc', None, 'tile'), may hold values from -6 to 6
- flux_pool: float32 [4, 2, 3, 8, 64, 128], P('trc', None, None, None, 'tile'), may hold values from -0.45 to 0.45
- mass_pool: float32 [4, 2, 8, 64, 128], P('trc', None, None, 'tile'), may hold values from 1 to 2
- owner: int32 [2, 8], P(None, 'tile'), may hold values from 0 to 3
- conv_cols: int32 [8, 256], P('tile'), may hold values from 0 to 1023, as said below
- conv_steps: int32 [8, 256], P('tile'), may hold values from 1 to 3
- conv_rate: float32 [8, 7, 256], P('tile'), may hold values from 0.05 to 0.5
Outputs:
- advected: float32 [16, 8, 64, 128], P('trc', None, 'tile')
Inputs may be any that keep to these rules, and one draw needn't show every extreme that they name: `conv_cols`: the 256 columns listed for one tile are all different.
All inputs are finite; a program needn't handle non-finite values.
Results may differ from a plain program's by a relative error of at most 0.0003.
Values sent between devices are 32-bit elements; how exact they have to be, the bound alone decides.
A program may use at most 64 MiB of HBM per device.

v0:
```python
import jax
import jax.numpy as jnp
from jax import lax
from jax.sharding import PartitionSpec as P


def padded_2(x, sides, width):
    for axis, dim in sides:
        size, length = (lax.axis_size(axis), x.shape[dim])
        up = [(i, (i + 1) % size) for i in range(size)]
        down = [(j, i) for i, j in up]
        last = lax.slice_in_dim(x, length - width, length, axis=dim)
        initial = lax.slice_in_dim(x, 0, width, axis=dim)
        before = lax.ppermute(last, axis, up)
        after = lax.ppermute(initial, axis, down)
        x = jnp.concatenate([before, x, after], axis=dim)
    return x


def slab(values_in, first_index, how_many, along):
    position = along % values_in.ndim
    return lax.slice_in_dim(values_in, first_index, first_index + how_many, axis=position)


def pad_axis(values_in, along, pad_low, pad_high, pad_mode):
    widths = [(0, 0)] * values_in.ndim
    widths[along % values_in.ndim] = (pad_low, pad_high)
    return jnp.pad(values_in, widths, mode=pad_mode)


def closed_faces(face_flux, along):
    position = along % face_flux.ndim
    face_count = face_flux.shape[position]
    dims_shape = [1] * face_flux.ndim
    dims_shape[position] = face_count
    kept_mask = (jnp.arange(face_count) < face_count - 1).reshape(dims_shape)
    return jnp.where(kept_mask, face_flux, 0.0)


def parabola_sweep(padded, mass_pad, face_flux, along, length):
    count_edges = length + 3
    outer_left = slab(padded, 0, count_edges, along)
    inner_left = slab(padded, 1, count_edges, along)
    inner_right = slab(padded, 2, count_edges, along)
    outer_right = slab(padded, 3, count_edges, along)
    edge_values = 7.0 / 12.0 * (inner_left + inner_right) - 1.0 / 12.0 * (outer_left + outer_right)
    edge_values = jnp.clip(
        edge_values, jnp.minimum(inner_left, inner_right), jnp.maximum(inner_left, inner_right)
    )
    count_cells = length + 2
    centre = slab(padded, 2, count_cells, along)
    left_edge = slab(edge_values, 0, count_cells, along)
    right_edge = slab(edge_values, 1, count_cells, along)
    extremum = (right_edge - centre) * (centre - left_edge) <= 0.0
    left_edge = jnp.where(extremum, centre, left_edge)
    right_edge = jnp.where(extremum, centre, right_edge)
    edge_jump = right_edge - left_edge
    curvature = 6.0 * (centre - 0.5 * (left_edge + right_edge))
    new_left = jnp.where(
        edge_jump * curvature > edge_jump * edge_jump, 3.0 * centre - 2.0 * right_edge, left_edge
    )
    new_right = jnp.where(
        -edge_jump * edge_jump > edge_jump * curvature, 3.0 * centre - 2.0 * left_edge, right_edge
    )
    edge_jump = new_right - new_left
    curvature = 6.0 * (centre - 0.5 * (new_left + new_right))
    face_count = length + 1
    upwind_mass = slab(mass_pad, 0, face_count, along)
    downwind_mass = slab(mass_pad, 1, face_count, along)
    forward = jnp.maximum(face_flux, 0.0) / upwind_mass
    backward = jnp.maximum(-face_flux, 0.0) / downwind_mass
    from_left = slab(new_right, 0, face_count, along) - 0.5 * forward * (
        slab(edge_jump, 0, face_count, along)
        - (1.0 - forward * (2.0 / 3.0)) * slab(curvature, 0, face_count, along)
    )
    from_right = slab(new_left, 1, face_count, along) + 0.5 * backward * (
        slab(edge_jump, 1, face_count, along)
        + (1.0 - backward * (2.0 / 3.0)) * slab(curvature, 1, face_count, along)
    )
    transport = face_flux * jnp.where(face_flux > 0.0, from_left, from_right)
    interior = slab(padded, 3, length, along)
    air_mass = slab(mass_pad, 1, length, along)
    return (
        interior
        - (slab(transport, 1, length, along) - slab(transport, 0, length, along)) / air_mass
    )


def local_sweep(tracer, face_flux, air_mass, along):
    length = tracer.shape[along]
    return parabola_sweep(
        pad_axis(tracer, along, 3, 3, "edge"),
        pad_axis(air_mass, along, 1, 1, "edge"),
        pad_axis(closed_faces(face_flux, along), along, 1, 0, "constant"),
        along,
        length,
    )


def convect(columns, rates, level_axis):
    lower_levels = slab(columns, 0, columns.shape[level_axis] - 1, level_axis)
    moved = rates * lower_levels
    return (
        columns
        + pad_axis(moved, level_axis, 1, 0, "constant")
        - pad_axis(moved, level_axis, 0, 1, "constant")
    )


def dense_convection(column_ids, step_counts, rates, cell_total):
    dense_rates = jnp.zeros((rates.shape[0], cell_total), jnp.float32).at[:, column_ids].set(rates)
    dense_steps = jnp.zeros((cell_total,), jnp.int32).at[column_ids].set(step_counts)
    return (dense_rates, dense_steps)


def convect_device(state, dense_rates, dense_steps):
    flattened = state.reshape(state.shape[0], state.shape[1], -1)
    for substep in range(3):
        flattened = jnp.where(dense_steps > substep, convect(flattened, dense_rates, -2), flattened)
    return flattened.reshape(state.shape)


def body(tracers, flux_pool, mass_pool, owner, conv_cols, conv_steps, conv_rate):
    tracer_count = tracers.shape[0]
    cells_x = tracers.shape[2]
    steps_total = flux_pool.shape[1]
    dense_rates, dense_steps = dense_convection(
        conv_cols[0], conv_steps[0], conv_rate[0], tracers.shape[2] * tracers.shape[3]
    )
    group_index = lax.axis_index("trc")
    stacked = jnp.concatenate((flux_pool[0], mass_pool[0][:, None]), axis=1)
    owned = (owner[:, 0] == group_index).reshape(-1, 1, 1, 1, 1)
    all_met = lax.psum(jnp.where(owned, stacked, 0.0), "trc")
    state = tracers
    for moment in range(steps_total):
        meteo = all_met[moment]
        joined = jnp.concatenate((state, meteo[0][None], meteo[3][None]), axis=0)
        joined_halo = padded_2(joined, (("tile", 2),), 3)
        tracer_halo = joined_halo[:tracer_count]
        met_halo = joined_halo[tracer_count:]
        rim_width = 3
        x_flux = slab(met_halo[0], rim_width - 1, cells_x + 1, -2)
        mass_pad = slab(met_halo[1], rim_width - 1, cells_x + 2, -2)
        state = parabola_sweep(tracer_halo, mass_pad, x_flux, -2, cells_x)
        state = local_sweep(state, meteo[1], meteo[3], -1)
        state = local_sweep(state, meteo[2], meteo[3], -3)
        state = convect_device(state, dense_rates, dense_steps)
    return state


def solution(mesh):
    in_specs = (
        P("trc", None, "tile", None),
        P("trc", None, None, None, "tile", None),
        P("trc", None, None, "tile", None),
        P(None, "tile"),
        P("tile", None),
        P("tile", None),
        P("tile", None, None),
    )
    out_specs = P("trc", None, "tile", None)
    return jax.shard_map(body, mesh=mesh, in_specs=in_specs, out_specs=out_specs, check_vma=False)
```

profile of v0, /device:TPU:0, one launch (start us, length us, event | category | flops | bytes accessed | tf_op | source)
XLA Modules:
  0.0 75.7 jit_solution(18111110729969603263)
XLA Ops:
  6.5 0.7 copy-done.4
  7.2 1.8 %maximum_select_fusion = f32[2,4,8,8,128]{4,3,2,1,0:T(8,128)} fusion(f32[2,1,8,8,128]{4,3,2,1,0:T(8,128)} %bitcast.87, f32[2,3,8,8,128]{4,3,2,1,0:T(8,128)} %bitcast.86, pred[2]{0:T(512)(128)(4,1)S(1)} %compare_bitcast_fusion), kind=kLoop, calls=%fused_computation.50 | loop fusion | flops 131072 | bytes 524290 | tf_op jit(solution)/shard_map/jit(_where)/select_n | solution.py:133
  9.0 0.7 copy-done.3
  9.8 1.3 %scatter_custom_fusion.1 = f32[7,1024]{0,1:T(8,128)S(1)} fusion(s32[256]{0:T(256)S(1)} %bitcast.96, f32[]{:T(128)} %constant.21.clone.1, f32[1,7,256]{1,2,0:T(8,128)S(1)} %copy.333), kind=kCustom, calls=%fused_computation.93 | custom fusion | bytes 159748 | tf_op jit(solution)/shard_map/scatter | solution.py:111
  11.3 1.6 %scatter_custom_fusion = s32[1024]{0:T(1024)S(1)} fusion(s32[256]{0:T(256)S(1)} %bitcast.97, s32[256]{0:T(256)} %bitcast.98, s32[]{:T(128)} %constant.16.clone.1), kind=kCustom, calls=%fused_computation.279 | custom fusion | bytes 4608 | tf_op jit(solution)/shard_map/scatter | solution.py:112
  12.9 34.8 %all-reduce.18.cloned.1.call-done = f32[2,4,8,8,128]{4,3,2,1,0:T(8,128)} async-done(((f32[2,4,8,8,128]{4,3,2,1,0:T(8,128)}), f32[2,4,8,8,128]{4,3,2,1,0:T(8,128)}) %all-reduce.18.cloned.1.call-update) | async-done | bytes 262160 | tf_op jit(solution)/shard_map/psum | solution.py:133
  47.7 0.9 %fusion.109 = (f32[8,8,128]{2,1,0:T(8,128)S(1)}, f32[8,8,128]{2,1,0:T(8,128)S(1)}, f32[8,8,128]{2,1,0:T(8,128)S(1)}, f32[8,8,128]{2,1,0:T(8,128)S(1)}) fusion(f32[2,4,8,8,128]{4,3,2,1,0:T(8,128)} %all-reduce.18.cloned.1.call-done, pred[8]{0:T(512)(128)(4,1)S(1)} %iota_compare_fusion, pred[128]{0:T(512)(128)(4,1)S(1)} %iota_compare_fusion.1), kind=kLoop, calls=%fused_computation.236 | loop fusion | flops 32768 | bytes 262280 | tf_op jit(solution)/shard_map/jit(_where)/select_n | solution.py:37
  49.0 0.8 %copy-done = f32[4,8,8,128]{3,2,1,0:T(8,128)S(1)} copy-done((f32[4,8,8,128]{3,2,1,0:T(8,128)S(1)}, f32[4,8,8,128]{3,2,1,0:T(8,128)}, u32[]{:S(2)}) %copy-start) | copy-done | bytes 131096
  49.9 0.5 collective-permute-start.1
  51.4 4.1 %collective-permute-done = f32[6,8,3,128]{3,1,2,0:T(8,128)S(1)} collective-permute-done((f32[6,8,3,128]{3,1,2,0:T(8,128)S(1)}, f32[6,8,3,128]{3,1,2,0:T(8,128)S(1)}, u32[]{:S(2)}, u32[]{:S(2)}) %collective-permute-start) | collective-permute-done | bytes 73760 | tf_op jit(solution)/shard_map/ppermute | solution.py:14
  56.3 0.3 copy.329
  57.0 0.3 fusion.39
  57.3 0.3 fusion.119
  57.7 0.3 fusion.32
  58.4 0.3 fusion.118
  59.5 2.7 %collective-permute-start.3 = (f32[6,8,3,128]{3,1,2,0:T(8,128)S(1)}, f32[6,8,3,128]{3,1,2,0:T(8,128)S(1)}, u32[]{:S(2)}, u32[]{:S(2)}) collective-permute-start(f32[6,8,3,128]{3,1,2,0:T(8,128)S(1)} %get-tuple-element.44), channel_id=1, source_target_pairs={{4,0},{8,4},{12,8},{16,12},{20,16},{24,20},{28,24},{0,28},{5,1},{9... | collective-permute-start | bytes 221192 | tf_op jit(solution)/shard_map/ppermute | solution.py:15
  62.2 2.3 %collective-permute-done.2 = f32[6,8,3,128]{3,1,2,0:T(8,128)S(1)} collective-permute-done((f32[6,8,3,128]{3,1,2,0:T(8,128)S(1)}, f32[6,8,3,128]{3,1,2,0:T(8,128)S(1)}, u32[]{:S(2)}, u32[]{:S(2)}) %collective-permute-start.2) | collective-permute-done | bytes 73760 | tf_op jit(solution)/shard_map/ppermute | solution.py:14
  65.1 0.2 copy.330
  65.4 0.3 copy.331
  66.0 0.3 fusion.47
  66.3 0.3 fusion.116
  66.8 0.3 fusion.16
  67.4 0.3 fusion.115
  68.2 0.7 copy.327
  (131 shorter events, 5.6 us)
Async XLA Ops:
  6.5 41.2 %all-reduce.18.cloned.1.call-start = ((), (), s32[]{:S(2)}) async-start(), calls=%async_computation | async-start | bytes 524288 | tf_op jit(solution)/shard_map/psum | solution.py:133
  6.5 0.7 copy-start.4
  9.0 0.7 copy-start.2
  9.0 0.7 copy-start.3
  47.7 1.1 %copy-start.1 = (f32[2,4,8,8,128]{4,3,2,1,0:T(8,128)S(1)}, f32[2,4,8,8,128]{4,3,2,1,0:T(8,128)}, u32[]{:S(2)}) copy-start(f32[2,4,8,8,128]{4,3,2,1,0:T(8,128)} %all-reduce.18.cloned.1.call-done) | copy-start | bytes 786436
  48.9 0.9 %copy-start = (f32[4,8,8,128]{3,2,1,0:T(8,128)S(1)}, f32[4,8,8,128]{3,2,1,0:T(8,128)}, u32[]{:S(2)}) copy-start(f32[4,8,8,128]{3,2,1,0:T(8,128)} %param.7) | copy-start | bytes 393220
  49.9 5.6 %collective-permute-start.1 = (f32[6,8,3,128]{3,1,2,0:T(8,128)S(1)}, f32[6,8,3,128]{3,1,2,0:T(8,128)S(1)}, u32[]{:S(2)}, u32[]{:S(2)}) collective-permute-start(f32[6,8,3,128]{3,1,2,0:T(8,128)S(1)} %get-tuple-element.46), channel_id=1, source_target_pairs={{4,0},{8,4},{12,8},{16,12},{20,16},{24,20},{28,24},{0,28},{5,1},{9... | collective-permute-start | bytes 221192 | tf_op jit(solution)/shard_map/ppermute | solution.py:15
  50.4 5.1 %collective-permute-start = (f32[6,8,3,128]{3,1,2,0:T(8,128)S(1)}, f32[6,8,3,128]{3,1,2,0:T(8,128)S(1)}, u32[]{:S(2)}, u32[]{:S(2)}) collective-permute-start(f32[6,8,3,128]{3,1,2,0:T(8,128)S(1)} %get-tuple-element.45), channel_id=1, source_target_pairs={{0,4},{4,8},{8,12},{12,16},{16,20},{20,24},{24,28},{28,0},{1,5},{5... | collective-permute-start | bytes 221192 | tf_op jit(solution)/shard_map/ppermute | solution.py:14
  59.3 5.2 %collective-permute-start.2 = (f32[6,8,3,128]{3,1,2,0:T(8,128)S(1)}, f32[6,8,3,128]{3,1,2,0:T(8,128)S(1)}, u32[]{:S(2)}, u32[]{:S(2)}) collective-permute-start(f32[6,8,3,128]{3,1,2,0:T(8,128)S(1)} %get-tuple-element.43), channel_id=1, source_target_pairs={{0,4},{4,8},{8,12},{12,16},{16,20},{20,24},{24,28},{28,0},{1,5},{5... | collective-permute-start | bytes 221192 | tf_op jit(solution)/shard_map/ppermute | solution.py:14
  59.5 5.1 %collective-permute-start.3 = (f32[6,8,3,128]{3,1,2,0:T(8,128)S(1)}, f32[6,8,3,128]{3,1,2,0:T(8,128)S(1)}, u32[]{:S(2)}, u32[]{:S(2)}) collective-permute-start(f32[6,8,3,128]{3,1,2,0:T(8,128)S(1)} %get-tuple-element.44), channel_id=1, source_target_pairs={{4,0},{8,4},{12,8},{16,12},{20,16},{24,20},{28,24},{0,28},{5,1},{9... | collective-permute-start | bytes 221192 | tf_op jit(solution)/shard_map/ppermute | solution.py:15
Sparse Core Ops, SparseCore 0:
  9.7 37.9 all-reduce.17
where the time goes:
time: 75.9 us; the launch traced here: 75.7 us
  waiting for transfers between devices  41.3 us (54%)
  between operations  14.3 us (19%)
  local copies, waits for them, and re-layouts  8.64 us (11%)
  other arithmetic  8.16 us (11%)
  starting transfers between devices  3.3 us (4%)
    psum x1, waiting for transfers between devices, body(): all_met = lax.psum(jnp.where(owned, stacked, 0.0), 'trc')  34.8 us
    ppermute x2, waiting for transfers between devices, padded_2(): before = lax.ppermute(last, axis, up)  6.47 us
    ppermute x2, starting transfers between devices, padded_2(): after = lax.ppermute(initial, axis, down)  3.17 us
    unnamed x19, local copies, waits for them, and re-layouts  2.31 us
    select_n x1, other arithmetic, body(): all_met = lax.psum(jnp.where(owned, stacked, 0.0), 'trc')  1.76 us
    scatter x1, local copies, waits for them, and re-layouts, dense_convection(): jnp.zeros((cell_total,), jnp.int32).at[column_ids].set(step_counts)  1.57 us
  transfers between devices with their start and end apart: 5, of which 3 were waited for; matrix products, arithmetic and copies ran while one was open for 5% of the time, Pallas kernels for 0%

commit v1 on v0

v1 whole, which is shorter than its diff:
```python
import functools

import jax
import jax.numpy as jnp
from jax import lax
from jax.experimental import pallas as pl
from jax.experimental.pallas import tpu as pltpu
from jax.sharding import PartitionSpec as P

FIELDS = 4
HALO = 3
SUBSTEPS = 3


def face_terms(flux, left_inverse, right_inverse):
    share = jnp.abs(flux) * jnp.where(flux > 0.0, left_inverse, right_inverse)
    half = 0.5 * flux * share
    bent = half * (3.0 - 2.0 * share)
    return flux - half - bent, half - bent


def edge_rise(before, here, after):
    raw = 0.5 * here + (1.0 / 12.0) * (before - after)
    return jnp.clip(raw, jnp.minimum(here, 0.0), jnp.maximum(here, 0.0))


def limited(up, down):
    up2 = up + up
    down2 = down + down
    right = jnp.clip(up, jnp.minimum(down2, 0.0), jnp.maximum(down2, 0.0))
    left = -jnp.clip(down, jnp.minimum(up2, 0.0), jnp.maximum(up2, 0.0))
    return right, left


def transport(flux, near, far, q0, right0, left0, q1, right1, left1):
    ahead = flux > 0.0
    return (
        flux * jnp.where(ahead, q0, q1)
        + near * jnp.where(ahead, right0, left1)
        + far * jnp.where(ahead, left0, right1)
    )


def kernel(
    dims,
    owner_ref, cols_ref, counts_ref, rate_ref, tracer_hbm, flux_hbm, mass_hbm,
    out_ref,
    own, inbox, relay, met, state, swept, halo_out, halo_in, rim_out, rim_in,
    cx, cy, cz, inverse_t, inverse_o, lift,
    own_sem, state_sem, chain_send, chain_recv, halo_send, halo_recv, rim_send, rim_recv,
):
    tiles, groups, steps, tracers, levels, cells, lats = dims
    rows = levels * cells
    tile = lax.axis_index("tile")
    me = lax.axis_index("trc")
    right = lax.rem(tile + 1, tiles)
    left = lax.rem(tile + tiles - 1, tiles)
    near = lax.div(2 * me, groups)
    far = 1 - near
    near_to = me + 1 - 2 * near
    far_to = me - 1 + 2 * near
    at_end = jnp.logical_or(me == 0, me == groups - 1)
    inner = jnp.logical_and(me > 0, me < groups - 1)
    chunk_total = steps * FIELDS

    load_state = pltpu.make_async_copy(tracer_hbm, state, state_sem)
    load_state.start()
    loads = []
    for s in range(steps):
        base = s * FIELDS * rows
        loads.append(pltpu.make_async_copy(
            mass_hbm.at[pl.ds(s * rows, rows)], own.at[pl.ds(base, rows)], own_sem.at[2 * s]))
        loads.append(pltpu.make_async_copy(
            flux_hbm.at[pl.ds(s * 3 * rows, 3 * rows)], own.at[pl.ds(base + rows, 3 * rows)],
            own_sem.at[2 * s + 1]))
    for load in loads:
        load.start()

    barrier = pltpu.get_barrier_semaphore()
    for neighbour in (left, right):
        pl.semaphore_signal(barrier, inc=1, device_id={"tile": neighbour}, device_id_type=pl.DeviceIdType.MESH)

    @pl.when(me > 0)
    def _():
        pl.semaphore_signal(barrier, inc=1, device_id={"trc": me - 1}, device_id_type=pl.DeviceIdType.MESH)

    @pl.when(me < groups - 1)
    def _():
        pl.semaphore_signal(barrier, inc=1, device_id={"trc": me + 1}, device_id_type=pl.DeviceIdType.MESH)

    def cell_rows(base, x):
        return pl.ds(base + x, levels, stride=cells)

    def block(i, size):
        return pl.ds(pl.multiple_of(i * size, size), size)

    cols = cols_ref[...]
    x_start = jnp.zeros_like(cols)
    for x in range(1, cells):
        x_start += jnp.where(cols >= x * lats, lats, 0)
    listed = cols.shape[1]
    at_x = x_start == lax.broadcasted_iota(jnp.int32, (cells, listed), 0) * lats
    at_y = ((cols - x_start) == lax.broadcasted_iota(jnp.int32, (lats, listed), 0)).astype(jnp.float32)
    spread = [jnp.where(at_x, counts_ref[...].astype(jnp.float32), 0.0)]
    for k in range(levels - 1):
        spread.append(jnp.where(at_x, rate_ref[pl.ds(k, 1), :], 0.0))
    dense = lax.dot_general(
        jnp.concatenate(spread, axis=0), at_y, (((1,), (1,)), ((), ())),
        precision=lax.Precision.HIGHEST, preferred_element_type=jnp.float32)
    count = dense[:cells]
    for n in range(SUBSTEPS):
        for k in range(levels - 1):
            lift[pl.ds((n * (levels - 1) + k) * cells, cells), :] = jnp.where(
                count > n + 0.5, dense[(k + 1) * cells:(k + 2) * cells], 0.0)

    def pack_halo(s, t, source, base):
        for i in range(HALO):
            at = (t * HALO + i) * levels
            halo_out[s, 0, pl.ds(at, levels), :] = source[cell_rows(base, cells - HALO + i), :]
            halo_out[s, 1, pl.ds(at, levels), :] = source[cell_rows(base, i), :]

    def halo_copy(s, side, t, how_many):
        size = HALO * levels
        at = pl.ds(pl.multiple_of(t * size, size), how_many * size)
        return pltpu.make_async_remote_copy(
            src_ref=halo_out.at[s, side, at], dst_ref=halo_in.at[s, side, at],
            send_sem=halo_send.at[s, side, t], recv_sem=halo_recv.at[s, side, t],
            device_id={"tile": left if side else right}, device_id_type=pl.DeviceIdType.MESH)

    load_state.wait()
    for t in range(tracers):
        pack_halo(0, t, state, t * rows)
    for load in loads:
        load.wait()

    expected = 2 + jnp.where(me > 0, 1, 0) + jnp.where(me < groups - 1, 1, 0)
    pl.semaphore_wait(barrier, expected)

    def raw(c):
        s, field = divmod(c, FIELDS)
        if field == 0:
            return mass_hbm.at[pl.ds(s * rows, rows)]
        return flux_hbm.at[pl.ds((s * 3 + field - 1) * rows, rows)]

    def chain_copy(c, way, to, source):
        at = pl.ds(c * rows, rows)
        return pltpu.make_async_remote_copy(
            src_ref=relay.at[way, at] if source is None else source, dst_ref=inbox.at[way, at],
            send_sem=chain_send.at[way, c], recv_sem=chain_recv.at[way, c],
            device_id={"trc": to}, device_id_type=pl.DeviceIdType.MESH)

    @pl.when(at_end)
    def _():
        for c in range(chunk_total):
            chain_copy(c, near, near_to, raw(c)).start()

    for side in (0, 1):
        halo_copy(0, side, 0, tracers).start()

    def owner_of(s):
        return jnp.full((rows, lats), owner_ref[s, 0], jnp.int32)

    def pass_on(c, way, to):
        at = pl.ds(c * rows, rows)
        relay[way, at, :] = jnp.where(owner_of(c // FIELDS) == me, own[at, :], inbox[way, at, :])
        chain_copy(c, way, to, None).start()

    def near_step(c):
        @pl.when(inner)
        def _():
            chain_copy(c, near, near_to, None).wait_recv()
            pass_on(c, near, near_to)

    def far_step(c):
        chain_copy(c, far, near_to, None).wait_recv()

        @pl.when(inner)
        def _():
            pass_on(c, far, far_to)

        at = pl.ds(c * rows, rows)
        holder = owner_of(c // FIELDS)
        met[at, :] = jnp.where(
            holder == me, own[at, :], jnp.where(holder < me, inbox[0, at, :], inbox[1, at, :]))

    def rim_copy(s, side):
        at = pl.ds(0, 2 * levels) if side == 0 else pl.ds(2 * levels, levels)
        return pltpu.make_async_remote_copy(
            src_ref=rim_out.at[s, at], dst_ref=rim_in.at[s, at],
            send_sem=rim_send.at[s, side], recv_sem=rim_recv.at[s, side],
            device_id={"tile": left if side else right}, device_id_type=pl.DeviceIdType.MESH)

    def start_rim(s):
        mass_at = s * FIELDS * rows
        rim_out[s, pl.ds(0, levels), :] = met[cell_rows(mass_at + rows, cells - 1), :]
        rim_out[s, pl.ds(levels, levels), :] = met[cell_rows(mass_at, cells - 1), :]
        rim_out[s, pl.ds(2 * levels, levels), :] = met[cell_rows(mass_at, 0), :]
        rim_copy(s, 0).start()
        rim_copy(s, 1).start()

    def x_terms(s):
        mass_at = s * FIELDS * rows
        inverses = [1.0 / rim_in[s, pl.ds(levels, levels), :]]
        fluxes = [rim_in[s, pl.ds(0, levels), :]]
        for x in range(cells):
            inverses.append(1.0 / met[cell_rows(mass_at, x), :])
            fluxes.append(met[cell_rows(mass_at + rows, x), :])
            inverse_t[pl.ds(x * levels, levels), :] = inverses[-1]
        inverses.append(1.0 / rim_in[s, pl.ds(2 * levels, levels), :])
        for x in range(cells + 1):
            at = pl.ds(x * levels, levels)
            cx[0, at, :] = fluxes[x]
            cx[1, at, :], cx[2, at, :] = face_terms(fluxes[x], inverses[x], inverses[x + 1])

    def y_terms(s):
        flux_at = (s * FIELDS + 2) * rows
        open_face = lax.broadcasted_iota(jnp.int32, (levels, lats), 1) < lats - 1
        for x in range(cells):
            at = pl.ds(x * levels, levels)
            flux = jnp.where(open_face, met[cell_rows(flux_at, x), :], 0.0)
            inverse = inverse_t[at, :]
            cy[0, at, :] = flux
            cy[1, at, :], cy[2, at, :] = face_terms(flux, inverse, pltpu.roll(inverse, lats - 1, 1))

    def z_terms(s):
        mass_at = s * FIELDS * rows
        flux_at = mass_at + 3 * rows
        inverses = []
        for k in range(levels):
            at = pl.ds(k * cells, cells)
            inverses.append(1.0 / met[pl.ds(mass_at + k * cells, cells), :])
            inverse_o[at, :] = inverses[-1]
        for k in range(levels - 1):
            at = pl.ds(k * cells, cells)
            flux = met[pl.ds(flux_at + k * cells, cells), :]
            cz[0, at, :] = flux
            cz[1, at, :], cz[2, at, :] = face_terms(flux, inverses[k], inverses[k + 1])

    def sweep_x(s, t):
        base = pl.multiple_of(t * rows, rows)
        q = []
        for i in range(HALO):
            q.append(halo_in[s, 0, block(t * HALO + i, levels), :])
        for x in range(cells):
            q.append(state[cell_rows(base, x), :])
        for i in range(HALO):
            q.append(halo_in[s, 1, block(t * HALO + i, levels), :])
        rise = [q[i + 1] - q[i] for i in range(cells + 5)]
        up = [edge_rise(rise[i], rise[i + 1], rise[i + 2]) for i in range(cells + 3)]
        shape = [limited(up[i + 1], rise[i + 1] - up[i]) for i in range(cells + 2)]
        moved = []
        for j in range(cells + 1):
            at = pl.ds(j * levels, levels)
            moved.append(transport(
                cx[0, at, :], cx[1, at, :], cx[2, at, :],
                q[j + 2], *shape[j], q[j + 3], *shape[j + 1]))
        return [
            q[x + 3] - (moved[x + 1] - moved[x]) * inverse_t[pl.ds(x * levels, levels), :]
            for x in range(cells)
        ]

    def sweep_y(x, q):
        at = pl.ds(x * levels, levels)
        inside = lax.broadcasted_iota(jnp.int32, (levels, lats), 1) < lats - 1

        def ahead(v):
            return pltpu.roll(v, lats - 1, 1)

        def behind(v):
            return pltpu.roll(v, 1, 1)

        q1 = ahead(q)
        rise = jnp.where(inside, q1 - q, 0.0)
        up = edge_rise(behind(rise), rise, ahead(rise))
        r, l = limited(up, behind(rise - up))
        moved = transport(cy[0, at, :], cy[1, at, :], cy[2, at, :], q, r, l, q1, ahead(r), ahead(l))
        return q - (moved - behind(moved)) * inverse_t[at, :]

    def sweep_xy(s, t):
        base = pl.multiple_of(t * rows, rows)
        after_x = sweep_x(s, t)
        for x in range(cells):
            swept[cell_rows(base, x), :] = sweep_y(x, after_x[x])

    def sweep_z(s, t):
        base = pl.multiple_of(t * rows, rows)
        q = [swept[pl.ds(base + k * cells, cells), :] for k in range(levels)]
        zero = jnp.zeros_like(q[0])
        rise = [zero] + [q[k + 1] - q[k] for k in range(levels - 1)] + [zero]
        up = [zero] + [edge_rise(rise[k], rise[k + 1], rise[k + 2]) for k in range(levels - 1)]
        shape = [(zero, zero)]
        for k in range(1, levels - 1):
            shape.append(limited(up[k + 1], rise[k] - up[k]))
        shape.append((zero, zero))
        moved = [zero]
        for k in range(levels - 1):
            at = pl.ds(k * cells, cells)
            moved.append(transport(
                cz[0, at, :], cz[1, at, :], cz[2, at, :], q[k], *shape[k], q[k + 1], *shape[k + 1]))
        moved.append(zero)
        q = [
            q[k] - (moved[k + 1] - moved[k]) * inverse_o[pl.ds(k * cells, cells), :]
            for k in range(levels)
        ]
        for n in range(SUBSTEPS):
            gain = [
                lift[pl.ds((n * (levels - 1) + k) * cells, cells), :] * q[k] for k in range(levels - 1)
            ]
            q = [
                (q[k] + gain[k - 1] if k else q[k]) - (gain[k] if k < levels - 1 else 0.0)
                for k in range(levels)
            ]
        target = out_ref if s == steps - 1 else state
        for k in range(levels):
            target[pl.ds(base + k * cells, cells), :] = q[k]

    def each_tracer(body):
        lax.fori_loop(0, tracers, lambda t, carry: (body(t), carry)[1], 0)

    def after_far(c):
        s, field = divmod(c, FIELDS)
        if field == 1:
            start_rim(s)
        if field == 2:
            rim_copy(s, 0).wait_recv()
            rim_copy(s, 1).wait_recv()
            x_terms(s)
            y_terms(s)
            if s == 0:
                for side in (0, 1):
                    halo_copy(0, side, 0, tracers).wait_recv()

            def xy(t):
                if s > 0:
                    for side in (0, 1):
                        halo_copy(s, side, t, 1).wait_recv()
                sweep_xy(s, t)

            each_tracer(xy)
        if field == 3:
            z_terms(s)

            def z(t):
                sweep_z(s, t)
                if s < steps - 1:
                    pack_halo(s + 1, t, state, pl.multiple_of(t * rows, rows))
                    for side in (0, 1):
                        halo_copy(s + 1, side, t, 1).start()

            each_tracer(z)

    near_step(0)
    for c in range(chunk_total):
        if c + 1 < chunk_total:
            near_step(c + 1)
        far_step(c)
        after_far(c)

    for side in (0, 1):
        halo_copy(0, side, 0, tracers).wait_send()
        for s in range(steps):
            rim_copy(s, side).wait_send()
    for s in range(1, steps):
        def left_device(t):
            for side in (0, 1):
                halo_copy(s, side, t, 1).wait_send()
        each_tracer(left_device)
    for c in range(chunk_total):
        chain_copy(c, near, near_to, None).wait_send()

    @pl.when(inner)
    def _():
        for c in range(chunk_total):
            chain_copy(c, far, far_to, None).wait_send()


def body(dims, tracers, flux_pool, mass_pool, owner, conv_cols, conv_steps, conv_rate):
    _, _, steps, count, levels, cells, lats = dims
    rows = levels * cells
    total = steps * FIELDS
    flat = (count * rows, lats)
    vmem = pl.BlockSpec(memory_space=pltpu.VMEM)
    hbm = pl.BlockSpec(memory_space=pl.ANY)
    f32 = jnp.float32
    out = pl.pallas_call(
        functools.partial(kernel, dims),
        out_shape=jax.ShapeDtypeStruct(flat, f32),
        in_specs=[pl.BlockSpec(memory_space=pltpu.SMEM), vmem, vmem, vmem, hbm, hbm, hbm],
        out_specs=vmem,
        scratch_shapes=[
            pltpu.VMEM((total * rows, lats), f32),
            pltpu.VMEM((2, total * rows, lats), f32),
            pltpu.VMEM((2, total * rows, lats), f32),
            pltpu.VMEM((total * rows, lats), f32),
            pltpu.VMEM(flat, f32),
            pltpu.VMEM(flat, f32),
            pltpu.VMEM((steps, 2, count * HALO * levels, lats), f32),
            pltpu.VMEM((steps, 2, count * HALO * levels, lats), f32),
            pltpu.VMEM((steps, 3 * levels, lats), f32),
            pltpu.VMEM((steps, 3 * levels, lats), f32),
            pltpu.VMEM((3, (cells + 1) * levels, lats), f32),
            pltpu.VMEM((3, rows, lats), f32),
            pltpu.VMEM((3, (levels - 1) * cells, lats), f32),
            pltpu.VMEM((rows, lats), f32),
            pltpu.VMEM((rows, lats), f32),
            pltpu.VMEM((SUBSTEPS * (levels - 1) * cells, lats), f32),
            pltpu.SemaphoreType.DMA((2 * steps,)),
            pltpu.SemaphoreType.DMA,
            pltpu.SemaphoreType.DMA((2, total)),
            pltpu.SemaphoreType.DMA((2, total)),
            pltpu.SemaphoreType.DMA((steps, 2, count)),
            pltpu.SemaphoreType.DMA((steps, 2, count)),
            pltpu.SemaphoreType.DMA((steps, 2)),
            pltpu.SemaphoreType.DMA((steps, 2)),
        ],
        compiler_params=pltpu.CompilerParams(collective_id=0, has_side_effects=True),
    )(
        owner, conv_cols, conv_steps, conv_rate[0], tracers.reshape(flat),
        flux_pool.reshape(steps * 3 * rows, lats), mass_pool.reshape(steps * rows, lats),
    )
    return out.reshape(tracers.shape)


def solution(mesh):
    def local(tracers, flux_pool, *rest):
        dims = (mesh.shape["tile"], mesh.shape["trc"], flux_pool.shape[1]) + tracers.shape
        return body(dims, tracers, flux_pool, *rest)

    in_specs = (
        P("trc", None, "tile", None),
        P("trc", None, None, None, "tile", None),
        P("trc", None, None, "tile", None),
        P(None, "tile"),
        P("tile", None),
        P("tile", None),
        P("tile", None, None),
    )
    out_specs = P("trc", None, "tile", None)
    return jax.shard_map(local, mesh=mesh, in_specs=in_specs, out_specs=out_specs, check_vma=False)
```

time: 75.9 us -> 32.1 us (0.42)
  waiting for transfers between devices: 41.3 us -> 0 us
  Pallas kernels: 0 us -> 28 us
  between operations: 14.3 us -> 0.01 us
  other arithmetic: 8.16 us -> 0 us
  local copies, waits for them, and re-layouts: 8.64 us -> 3.5 us
  starting transfers between devices: 3.3 us -> 0 us
    psum x1 -> x0, waiting for transfers between devices: 34.8 us -> none  [body(): all_met = lax.psum(jnp.where(owned, stacked, 0.0), 'trc')]
    pallas_call x0 -> x1, Pallas kernels: none -> 28 us  [body(): pl.pallas_call(functools.partial(kernel, dims), out_shape=jax.ShapeDtypeS...]
    ppermute x4 -> x0, waiting for transfers between devices: 6.47 us -> none  [the longest x2 6.47 us: padded_2(): before = lax.ppermute(last, axis, up)]
    ppermute x4 -> x0, starting transfers between devices: 3.3 us -> none  [the longest x2 3.17 us: padded_2(): after = lax.ppermute(initial, axis, down)]
    scatter x3 -> x0, local copies, waits for them, and re-layouts: 3.05 us -> none  [the longest x1 1.57 us: dense_convection(): jnp.zeros((cell_total,), jnp.int32).at[column_ids].set(step_counts)]
    select_n x7 -> x0, other arithmetic: 2.83 us -> none  [the longest x1 1.76 us: body(): all_met = lax.psum(jnp.where(owned, stacked, 0.0), 'trc')]
    mul x24 -> x0, other arithmetic: 1.89 us -> none  [the longest x6 1 us: parabola_sweep(): transport = face_flux * jnp.where(face_flux > 0.0, from_left, from_right)]
    sub x10 -> x0, other arithmetic: 1.67 us -> none  [the longest x6 1.37 us: parabola_sweep(): edge_jump = new_right - new_left]
  transfers between devices with their start and end apart: 5 -> 0, of which waited for: 3 -> 0; matrix products, arithmetic and copies ran while one was open for 5% -> 0% of each run, Pallas kernels for 0% -> 0%
where the time goes in v1:
time: 32.1 us; the launch traced here: 31.5 us
  Pallas kernels  28 us (87%)
  local copies, waits for them, and re-layouts  3.5 us (11%)
    pallas_call x1, Pallas kernels, body(): pl.pallas_call(functools.partial(kernel, dims), out_shape=jax.ShapeDtypeS...  28 us
    unnamed x5, local copies, waits for them, and re-layouts  3.5 us

profile of v1, /device:TPU:0, one launch (start us, length us, event | category | flops | bytes accessed | tf_op | source)
XLA Modules:
  0.0 31.5 jit_solution(13094075394933314840)
XLA Ops:
  0.0 0.0 copy-start
  0.0 1.3 %copy.8.owner_ref = s32[2,1]{1,0:T(2,128)} copy(s32[2,1]{0,1:T(1,128)} %param.10) | data formatting | bytes 16 | tf_op args[3]
  1.3 0.0 copy-done
  1.3 0.6 %copy.11 = f32[1,7,256]{2,1,0:T(8,128)} copy(f32[1,7,256]{2,0,1:T(1,128)S(1)} %copy-done) | data formatting | bytes 14336
  1.9 28.0 %shard_map.73 = f32[256,128]{1,0:T(8,128)} custom-call(s32[2,1]{1,0:T(2,128)} %copy.8.owner_ref, s32[1,256]{1,0:T(1,128)} %cols_ref.1, s32[1,256]{1,0:T(1,128)} %counts_ref.1, f32[7,256]{1,0:T(8,128)} %bitcast.11, f32[256,128]{1,0:T(8,128)} %bitcast.9, f32[384,128]{1,0:T(8,128)} %bitcast.8, f32[128,128]{1,0:T(8,128)} %bitcast.10), custom_call_target="tpu_custom_call" | custom-call | tf_op jit(solution)/shard_map/pallas_call | solution.py:385
  29.9 1.6 %copy.13 = f32[4,8,8,128]{3,2,1,0:T(8,128)} copy(f32[4,8,8,128]{3,2,1,0:T(8,128)} %bitcast.7) | data formatting | bytes 262144
Async XLA Ops:
  0.0 1.3 %copy-start = (f32[1,7,256]{2,0,1:T(1,128)S(1)}, f32[1,7,256]{2,0,1:T(1,128)}, u32[]{:S(2)}) copy-start(f32[1,7,256]{2,0,1:T(1,128)} %param.13) | copy-start | bytes 21508

commit v2 on v1

--- a/solution.py
+++ b/solution.py
@@ -10,6 +10,7 @@
 FIELDS = 4
 HALO = 3
 SUBSTEPS = 3
+LEAD = 2
 
 
 def face_terms(flux, left_inverse, right_inverse):
@@ -94,6 +95,51 @@
     def block(i, size):
         return pl.ds(pl.multiple_of(i * size, size), size)
 
+    def pack_halo(s, t, source, base):
+        for i in range(HALO):
+            at = (t * HALO + i) * levels
+            halo_out[s, 0, pl.ds(at, levels), :] = source[cell_rows(base, cells - HALO + i), :]
+            halo_out[s, 1, pl.ds(at, levels), :] = source[cell_rows(base, i), :]
+
+    def halo_copy(s, side, t, how_many):
+        size = HALO * levels
+        at = pl.ds(pl.multiple_of(t * size, size), how_many * size)
+        return pltpu.make_async_remote_copy(
+            src_ref=halo_out.at[s, side, at], dst_ref=halo_in.at[s, side, at],
+            send_sem=halo_send.at[s, side, t], recv_sem=halo_recv.at[s, side, t],
+            device_id={"tile": left if side else right}, device_id_type=pl.DeviceIdType.MESH)
+
+    load_state.wait()
+    for t in range(tracers):
+        pack_halo(0, t, state, t * rows)
+
+    expected = 2 + jnp.where(me > 0, 1, 0) + jnp.where(me < groups - 1, 1, 0)
+    pl.semaphore_wait(barrier, expected)
+
+    def raw(c):
+        s, field = divmod(c, FIELDS)
+        if field == 0:
+            return mass_hbm.at[pl.ds(s * rows, rows)]
+        return flux_hbm.at[pl.ds((s * 3 + field - 1) * rows, rows)]
+
+    def chunk(c):
+        return pl.ds(c * rows, rows) if isinstance(c, int) else block(c, rows)
+
+    def chain_copy(c, way, to, source=None):
+        at = chunk(c)
+        return pltpu.make_async_remote_copy(
+            src_ref=relay.at[way, at] if source is None else source, dst_ref=inbox.at[way, at],
+            send_sem=chain_send.at[way, c], recv_sem=chain_recv.at[way, c],
+            device_id={"trc": to}, device_id_type=pl.DeviceIdType.MESH)
+
+    @pl.when(at_end)
+    def _():
+        for c in range(chunk_total):
+            chain_copy(c, near, near_to, raw(c)).start()
+
+    for side in (0, 1):
+        halo_copy(0, side, 0, tracers).start()
+
     cols = cols_ref[...]
     x_start = jnp.zeros_like(cols)
     for x in range(1, cells):
@@ -103,7 +149,7 @@
     at_y = ((cols - x_start) == lax.broadcasted_iota(jnp.int32, (lats, listed), 0)).astype(jnp.float32)
     spread = [jnp.where(at_x, counts_ref[...].astype(jnp.float32), 0.0)]
     for k in range(levels - 1):
-        spread.append(jnp.where(at_x, rate_ref[pl.ds(k, 1), :], 0.0))
+        spread.append(jnp.where(at_x, rate_ref[k], 0.0))
     dense = lax.dot_general(
         jnp.concatenate(spread, axis=0), at_y, (((1,), (1,)), ((), ())),
         precision=lax.Precision.HIGHEST, preferred_element_type=jnp.float32)
@@ -113,75 +159,39 @@
             lift[pl.ds((n * (levels - 1) + k) * cells, cells), :] = jnp.where(
                 count > n + 0.5, dense[(k + 1) * cells:(k + 2) * cells], 0.0)
 
-    def pack_halo(s, t, source, base):
-        for i in range(HALO):
-            at = (t * HALO + i) * levels
-            halo_out[s, 0, pl.ds(at, levels), :] = source[cell_rows(base, cells - HALO + i), :]
-            halo_out[s, 1, pl.ds(at, levels), :] = source[cell_rows(base, i), :]
-
-    def halo_copy(s, side, t, how_many):
-        size = HALO * levels
-        at = pl.ds(pl.multiple_of(t * size, size), how_many * size)
-        return pltpu.make_async_remote_copy(
-            src_ref=halo_out.at[s, side, at], dst_ref=halo_in.at[s, side, at],
-            send_sem=halo_send.at[s, side, t], recv_sem=halo_recv.at[s, side, t],
-            device_id={"tile": left if side else right}, device_id_type=pl.DeviceIdType.MESH)
-
-    load_state.wait()
-    for t in range(tracers):
-        pack_halo(0, t, state, t * rows)
     for load in loads:
         load.wait()
 
-    expected = 2 + jnp.where(me > 0, 1, 0) + jnp.where(me < groups - 1, 1, 0)
-    pl.semaphore_wait(barrier, expected)
-
-    def raw(c):
-        s, field = divmod(c, FIELDS)
-        if field == 0:
-            return mass_hbm.at[pl.ds(s * rows, rows)]
-        return flux_hbm.at[pl.ds((s * 3 + field - 1) * rows, rows)]
-
-    def chain_copy(c, way, to, source):
-        at = pl.ds(c * rows, rows)
-        return pltpu.make_async_remote_copy(
-            src_ref=relay.at[way, at] if source is None else source, dst_ref=inbox.at[way, at],
-            send_sem=chain_send.at[way, c], recv_sem=chain_recv.at[way, c],
-            device_id={"trc": to}, device_id_type=pl.DeviceIdType.MESH)
-
-    @pl.when(at_end)
-    def _():
-        for c in range(chunk_total):
-            chain_copy(c, near, near_to, raw(c)).start()
-
-    for side in (0, 1):
-        halo_copy(0, side, 0, tracers).start()
-
     def owner_of(s):
-        return jnp.full((rows, lats), owner_ref[s, 0], jnp.int32)
-
-    def pass_on(c, way, to):
-        at = pl.ds(c * rows, rows)
-        relay[way, at, :] = jnp.where(owner_of(c // FIELDS) == me, own[at, :], inbox[way, at, :])
-        chain_copy(c, way, to, None).start()
-
-    def near_step(c):
+        return jnp.full((rows, lats), owner_ref[0, s], jnp.int32)
+
+    def pass_on(s, c, way, to):
+        at = chunk(c)
+        relay[way, at, :] = jnp.where(owner_of(s) == me, own[at, :], inbox[way, at, :])
+        chain_copy(c, way, to).start()
+
+    def near_step(s, c):
         @pl.when(inner)
         def _():
-            chain_copy(c, near, near_to, None).wait_recv()
-            pass_on(c, near, near_to)
-
-    def far_step(c):
-        chain_copy(c, far, near_to, None).wait_recv()
+            chain_copy(c, near, near_to).wait_recv()
+            pass_on(s, c, near, near_to)
+
+    def far_arrives(s, c):
+        chain_copy(c, far, near_to).wait_recv()
 
         @pl.when(inner)
         def _():
-            pass_on(c, far, far_to)
-
-        at = pl.ds(c * rows, rows)
-        holder = owner_of(c // FIELDS)
+            pass_on(s, c, far, far_to)
+
+    def choose(s, c):
+        at = chunk(c)
+        holder = owner_of(s)
         met[at, :] = jnp.where(
             holder == me, own[at, :], jnp.where(holder < me, inbox[0, at, :], inbox[1, at, :]))
+
+    def far_step(s, c):
+        far_arrives(s, c)
+        choose(s, c)
 
     def rim_copy(s, side):
         at = pl.ds(0, 2 * levels) if side == 0 else pl.ds(2 * levels, levels)
@@ -276,11 +286,11 @@
         moved = transport(cy[0, at, :], cy[1, at, :], cy[2, at, :], q, r, l, q1, ahead(r), ahead(l))
         return q - (moved - behind(moved)) * inverse_t[at, :]
 
-    def sweep_xy(s, t):
-        base = pl.multiple_of(t * rows, rows)
-        after_x = sweep_x(s, t)
+    def sweep_xy(s, some):
+        after_x = [sweep_x(s, t) for t in some]
         for x in range(cells):
-            swept[cell_rows(base, x), :] = sweep_y(x, after_x[x])
+            for t, q in zip(some, after_x):
+                swept[cell_rows(pl.multiple_of(t * rows, rows), x), :] = sweep_y(x, q[x])
 
     def sweep_z(s, t):
         base = pl.multiple_of(t * rows, rows)
@@ -314,64 +324,104 @@
         for k in range(levels):
             target[pl.ds(base + k * cells, cells), :] = q[k]
 
-    def each_tracer(body):
-        lax.fori_loop(0, tracers, lambda t, carry: (body(t), carry)[1], 0)
-
-    def after_far(c):
-        s, field = divmod(c, FIELDS)
-        if field == 1:
-            start_rim(s)
-        if field == 2:
-            rim_copy(s, 0).wait_recv()
-            rim_copy(s, 1).wait_recv()
-            x_terms(s)
-            y_terms(s)
-            if s == 0:
-                for side in (0, 1):
-                    halo_copy(0, side, 0, tracers).wait_recv()
-
-            def xy(t):
+    together = 2 if tracers % 2 == 0 else 1
+    loops = tracers // together
+
+    def each_group(body):
+        def run(p, carry):
+            body(p, [p * together + i for i in range(together)])
+            return carry
+        lax.fori_loop(0, loops, run, 0)
+
+    def halo_arrives(s, some):
+        for t in some:
+            for side in (0, 1):
+                halo_copy(s, side, t, 1).wait_recv()
+
+    def rim_arrives(s):
+        for side in (0, 1):
+            rim_copy(s, side).wait_recv()
+
+    def near_if(c):
+        if c < chunk_total:
+            near_step(c // FIELDS, c)
+
+    for c in range(LEAD):
+        near_if(c)
+    far_done = 0
+    for s in range(steps):
+        first = s * FIELDS
+        final = s == steps - 1
+        for c in range(far_done, first + FIELDS - final):
+            near_if(c + LEAD)
+            far_step(s, c)
+            if c == first + 1:
+                start_rim(s)
+        far_done = first + FIELDS
+        if final:
+            last = chunk_total - 1
+
+            @pl.when(inner)
+            def _():
+                far_arrives(s, last)
+
+        rim_arrives(s)
+        x_terms(s)
+        y_terms(s)
+        if s == 0:
+            for side in (0, 1):
+                halo_copy(0, side, 0, tracers).wait_recv()
+        if final:
+            def do_xy(p, some):
                 if s > 0:
-                    for side in (0, 1):
-                        halo_copy(s, side, t, 1).wait_recv()
-                sweep_xy(s, t)
-
-            each_tracer(xy)
-        if field == 3:
+                    halo_arrives(s, some)
+                sweep_xy(s, some)
+            each_group(do_xy)
+
+            @pl.when(at_end)
+            def _():
+                far_arrives(s, last)
+
+            choose(s, last)
             z_terms(s)
-
-            def z(t):
-                sweep_z(s, t)
-                if s < steps - 1:
+            each_group(lambda p, some: [sweep_z(s, t) for t in some])
+        else:
+            z_terms(s)
+            slots = loops if loops <= FIELDS - LEAD else 0
+
+            def do_all(p, some):
+                if s > 0:
+                    halo_arrives(s, some)
+                sweep_xy(s, some)
+                for t in some:
+                    sweep_z(s, t)
+                for t in some:
                     pack_halo(s + 1, t, state, pl.multiple_of(t * rows, rows))
                     for side in (0, 1):
                         halo_copy(s + 1, side, t, 1).start()
-
-            each_tracer(z)
-
-    near_step(0)
-    for c in range(chunk_total):
-        if c + 1 < chunk_total:
-            near_step(c + 1)
-        far_step(c)
-        after_far(c)
+                if slots:
+                    near_step(s + 1, far_done + LEAD + p)
+                    far_step(s + 1, far_done + p)
+            each_group(do_all)
+            if slots > 1:
+                start_rim(s + 1)
+            far_done += slots
 
     for side in (0, 1):
         halo_copy(0, side, 0, tracers).wait_send()
         for s in range(steps):
             rim_copy(s, side).wait_send()
     for s in range(1, steps):
-        def left_device(t):
+        for t in range(tracers):
             for side in (0, 1):
                 halo_copy(s, side, t, 1).wait_send()
-        each_tracer(left_device)
     for c in range(chunk_total):
-        chain_copy(c, near, near_to, None).wait_send()
+        chain_copy(c, near, near_to).wait_send()
 
     @pl.when(inner)
     def _():
         for c in range(chunk_total):
-            chain_copy(c, far, far_to, None).wait_send()
+            chain_copy(c, far, far_to).wait_send()
 
 
 def body(dims, tracers, flux_pool, mass_pool, owner, conv_cols, conv_steps, conv_rate):
@@ -415,7 +465,7 @@
         ],
         compiler_params=pltpu.CompilerParams(collective_id=0, has_side_effects=True),
     )(
-        owner, conv_cols, conv_steps, conv_rate[0], tracers.reshape(flat),
+        owner.T, conv_cols, conv_steps, jnp.transpose(conv_rate, (1, 0, 2)), tracers.reshape(flat),
         flux_pool.reshape(steps * 3 * rows, lats), mass_pool.reshape(steps * rows, lats),
     )
     return out.reshape(tracers.shape)

time: 32.1 us -> 27.1 us (0.84); the launches traced: 31.5 us -> 26.9 us
  Pallas kernels: 28 us -> 25.3 us
  local copies, waits for them, and re-layouts: 3.5 us -> 1.57 us
    pallas_call x1, Pallas kernels: 28 us -> 25.3 us  [body(): pl.pallas_call(functools.partial(kernel, dims), out_shape=jax.ShapeDtypeS...]
    unnamed x5 -> x1, local copies, waits for them, and re-layouts: 3.5 us -> 1.57 us
where the time goes in v2:
time: 27.1 us; the launch traced here: 26.9 us
  Pallas kernels  25.3 us (93%)
  local copies, waits for them, and re-layouts  1.57 us (6%)
    pallas_call x1, Pallas kernels, body(): pl.pallas_call(functools.partial(kernel, dims), out_shape=jax.ShapeDtypeS...  25.3 us
    unnamed x1, local copies, waits for them, and re-layouts  1.57 us

profile of v2, /device:TPU:0, one launch (start us, length us, event | category | flops | bytes accessed | tf_op | source)
XLA Modules:
  0.0 26.9 jit_solution(18126354355365509991)
XLA Ops:
  0.0 25.3 %shard_map.73 = f32[256,128]{1,0:T(8,128)} custom-call(s32[1,2]{1,0:T(1,128)} %bitcast.11, s32[1,256]{1,0:T(1,128)} %cols_ref.1, s32[1,256]{1,0:T(1,128)} %counts_ref.1, f32[7,1,256]{2,1,0:T(1,128)} %bitcast.10, f32[256,128]{1,0:T(8,128)} %bitcast.8, f32[384,128]{1,0:T(8,128)} %bitcast.7, f32[128,128]{1,0:T(8,128)} %bitcast.9), custom_call_target="tpu_custom_call" | custom-call | tf_op jit(solution)/shard_map/pallas_call | solution.py:435
  25.3 1.6 %copy.9 = f32[4,8,8,128]{3,2,1,0:T(8,128)} copy(f32[4,8,8,128]{3,2,1,0:T(8,128)} %bitcast.6) | data formatting | bytes 262144

commit v3 on v2

--- a/solution.py
+++ b/solution.py
@@ -46,7 +46,7 @@
     dims,
     owner_ref, cols_ref, counts_ref, rate_ref, tracer_hbm, flux_hbm, mass_hbm,
     out_ref,
-    own, inbox, relay, met, state, swept, halo_out, halo_in, rim_out, rim_in,
+    own, inbox, relay, met, state, mid, swept, shapes, halo_out, halo_in, rim_out, rim_in,
     cx, cy, cz, inverse_t, inverse_o, lift,
     own_sem, state_sem, chain_send, chain_recv, halo_send, halo_recv, rim_send, rim_recv,
 ):
@@ -208,14 +208,21 @@
         rim_copy(s, 0).start()
         rim_copy(s, 1).start()
 
+    def mass_terms(s):
+        mass_at = s * FIELDS * rows
+        for k in range(levels):
+            at = pl.ds(k * cells, cells)
+            inverse_o[at, :] = 1.0 / met[pl.ds(mass_at + k * cells, cells), :]
+        for x in range(cells):
+            inverse_t[pl.ds(x * levels, levels), :] = inverse_o[cell_rows(0, x), :]
+
     def x_terms(s):
         mass_at = s * FIELDS * rows
         inverses = [1.0 / rim_in[s, pl.ds(levels, levels), :]]
         fluxes = [rim_in[s, pl.ds(0, levels), :]]
         for x in range(cells):
-            inverses.append(1.0 / met[cell_rows(mass_at, x), :])
+            inverses.append(inverse_t[pl.ds(x * levels, levels), :])
             fluxes.append(met[cell_rows(mass_at + rows, x), :])
-            inverse_t[pl.ds(x * levels, levels), :] = inverses[-1]
         inverses.append(1.0 / rim_in[s, pl.ds(2 * levels, levels), :])
         for x in range(cells + 1):
             at = pl.ds(x * levels, levels)
@@ -233,41 +240,43 @@
             cy[1, at, :], cy[2, at, :] = face_terms(flux, inverse, pltpu.roll(inverse, lats - 1, 1))
 
     def z_terms(s):
-        mass_at = s * FIELDS * rows
-        flux_at = mass_at + 3 * rows
-        inverses = []
-        for k in range(levels):
-            at = pl.ds(k * cells, cells)
-            inverses.append(1.0 / met[pl.ds(mass_at + k * cells, cells), :])
-            inverse_o[at, :] = inverses[-1]
+        flux_at = (s * FIELDS + 3) * rows
         for k in range(levels - 1):
             at = pl.ds(k * cells, cells)
             flux = met[pl.ds(flux_at + k * cells, cells), :]
             cz[0, at, :] = flux
-            cz[1, at, :], cz[2, at, :] = face_terms(flux, inverses[k], inverses[k + 1])
-
-    def sweep_x(s, t):
+            cz[1, at, :], cz[2, at, :] = face_terms(
+                flux, inverse_o[at, :], inverse_o[pl.ds((k + 1) * cells, cells), :])
+
+    def padded_x(s, t):
         base = pl.multiple_of(t * rows, rows)
-        q = []
-        for i in range(HALO):
-            q.append(halo_in[s, 0, block(t * HALO + i, levels), :])
-        for x in range(cells):
-            q.append(state[cell_rows(base, x), :])
-        for i in range(HALO):
-            q.append(halo_in[s, 1, block(t * HALO + i, levels), :])
+        q = [halo_in[s, 0, block(t * HALO + i, levels), :] for i in range(HALO)]
+        q += [state[cell_rows(base, x), :] for x in range(cells)]
+        return q + [halo_in[s, 1, block(t * HALO + i, levels), :] for i in range(HALO)]
+
+    def shape_x(s, t):
+        q = padded_x(s, t)
         rise = [q[i + 1] - q[i] for i in range(cells + 5)]
         up = [edge_rise(rise[i], rise[i + 1], rise[i + 2]) for i in range(cells + 3)]
-        shape = [limited(up[i + 1], rise[i + 1] - up[i]) for i in range(cells + 2)]
+        for i in range(cells + 2):
+            at = block(t * (cells + 2) + i, levels)
+            shapes[0, at, :], shapes[1, at, :] = limited(up[i + 1], rise[i + 1] - up[i])
+
+    def sweep_x(s, t):
+        q = padded_x(s, t)
+        shape = []
+        for i in range(cells + 2):
+            at = block(t * (cells + 2) + i, levels)
+            shape.append((shapes[0, at, :], shapes[1, at, :]))
         moved = []
         for j in range(cells + 1):
             at = pl.ds(j * levels, levels)
             moved.append(transport(
                 cx[0, at, :], cx[1, at, :], cx[2, at, :],
                 q[j + 2], *shape[j], q[j + 3], *shape[j + 1]))
-        return [
-            q[x + 3] - (moved[x + 1] - moved[x]) * inverse_t[pl.ds(x * levels, levels), :]
-            for x in range(cells)
-        ]
+        for x in range(cells):
+            mid[block(t * cells + x, levels), :] = (
+                q[x + 3] - (moved[x + 1] - moved[x]) * inverse_t[pl.ds(x * levels, levels), :])
 
     def sweep_y(x, q):
         at = pl.ds(x * levels, levels)
@@ -286,11 +295,11 @@
         moved = transport(cy[0, at, :], cy[1, at, :], cy[2, at, :], q, r, l, q1, ahead(r), ahead(l))
         return q - (moved - behind(moved)) * inverse_t[at, :]
 
-    def sweep_xy(s, some):
-        after_x = [sweep_x(s, t) for t in some]
+    def sweep_ys(some):
         for x in range(cells):
-            for t, q in zip(some, after_x):
-                swept[cell_rows(pl.multiple_of(t * rows, rows), x), :] = sweep_y(x, q[x])
+            for t in some:
+                swept[cell_rows(pl.multiple_of(t * rows, rows), x), :] = sweep_y(
+                    x, mid[block(t * cells + x, levels), :])
 
     def sweep_z(s, t):
         base = pl.multiple_of(t * rows, rows)
@@ -346,66 +355,74 @@
         if c < chunk_total:
             near_step(c // FIELDS, c)
 
-    for c in range(LEAD):
-        near_if(c)
-    far_done = 0
-    for s in range(steps):
-        first = s * FIELDS
-        final = s == steps - 1
-        for c in range(far_done, first + FIELDS - final):
-            near_if(c + LEAD)
-            far_step(s, c)
-            if c == first + 1:
-                start_rim(s)
-        far_done = first + FIELDS
-        if final:
-            last = chunk_total - 1
-
-            @pl.when(inner)
-            def _():
-                far_arrives(s, last)
-
-        rim_arrives(s)
-        x_terms(s)
-        y_terms(s)
-        if s == 0:
-            for side in (0, 1):
-                halo_copy(0, side, 0, tracers).wait_recv()
-        if final:
-            def do_xy(p, some):
-                if s > 0:
-                    halo_arrives(s, some)
-                sweep_xy(s, some)
-            each_group(do_xy)
-
-            @pl.when(at_end)
-            def _():
-                far_arrives(s, last)
-
-            choose(s, last)
-            z_terms(s)
-            each_group(lambda p, some: [sweep_z(s, t) for t in some])
-        else:
-            z_terms(s)
-            slots = loops if loops <= FIELDS - LEAD else 0
-
-            def do_all(p, some):
-                if s > 0:
-                    halo_arrives(s, some)
-                sweep_xy(s, some)
-                for t in some:
-                    sweep_z(s, t)
+    def shape_xs(s):
+        each_group(lambda p, some: [shape_x(s, t) for t in some])
+
+    def sweep_xs(s):
+        each_group(lambda p, some: [sweep_x(s, t) for t in some])
+
+    def sweep_zs(s):
+        def run(p, some):
+            for t in some:
+                sweep_z(s, t)
+            if s < steps - 1:
                 for t in some:
                     pack_halo(s + 1, t, state, pl.multiple_of(t * rows, rows))
                     for side in (0, 1):
                         halo_copy(s + 1, side, t, 1).start()
-                if slots:
-                    near_step(s + 1, far_done + LEAD + p)
-                    far_step(s + 1, far_done + p)
-            each_group(do_all)
-            if slots > 1:
-                start_rim(s + 1)
-            far_done += slots
+        each_group(run)
+
+    def link(c):
+        s, field = divmod(c, FIELDS)
+        near_if(c + LEAD)
+        far_step(s, c)
+        if field == 0 and s == 0:
+            mass_terms(s)
+        if field == 1:
+            start_rim(s)
+
+    def links(start, stop):
+        for c in range(start, min(stop, chunk_total)):
+            link(c)
+
+    for side in (0, 1):
+        halo_copy(0, side, 0, tracers).wait_recv()
+    near_if(0)
+    shape_xs(0)
+    for c in range(1, LEAD):
+        near_if(c)
+    links(0, FIELDS - (steps == 1))
+    for s in range(steps):
+        follow = (s + 1) * FIELDS
+        last = chunk_total - 1
+        final = s == steps - 1
+        if s > 0:
+            links(follow - 2, follow - final)
+            mass_terms(s)
+        if final:
+            @pl.when(inner)
+            def _():
+                far_arrives(s, last)
+        if s > 0:
+            each_group(lambda p, some: halo_arrives(s, some))
+            shape_xs(s)
+        rim_arrives(s)
+        x_terms(s)
+        sweep_xs(s)
+        y_terms(s)
+        each_group(lambda p, some: sweep_ys(some))
+        if final:
+            @pl.when(at_end)
+            def _():
+                far_arrives(s, last)
+
+            choose(s, last)
+        else:
+            links(follow, follow + 1)
+        z_terms(s)
+        sweep_zs(s)
+        if not final:
+            links(follow + 1, follow + 2)
 
     for side in (0, 1):
         halo_copy(0, side, 0, tracers).wait_send()
@@ -444,6 +461,8 @@
             pltpu.VMEM((total * rows, lats), f32),
             pltpu.VMEM(flat, f32),
             pltpu.VMEM(flat, f32),
+            pltpu.VMEM(flat, f32),
+            pltpu.VMEM((2, count * (cells + 2) * levels, lats), f32),
             pltpu.VMEM((steps, 2, count * HALO * levels, lats), f32),
             pltpu.VMEM((steps, 2, count * HALO * levels, lats), f32),
             pltpu.VMEM((steps, 3 * levels, lats), f32),

time: 27.1 us -> 27.2 us (level)
  no operation moved by 1% of the time
where the time goes in v3:
time: 27.2 us; the launch traced here: 27 us
  Pallas kernels  25.4 us (93%)
  local copies, waits for them, and re-layouts  1.57 us (6%)
    pallas_call x1, Pallas kernels, body(): pl.pallas_call(functools.partial(kernel, dims), out_shape=jax.ShapeDtypeS...  25.4 us
    unnamed x1, local copies, waits for them, and re-layouts  1.57 us

profile of v3, /device:TPU:0, one launch (start us, length us, event | category | flops | bytes accessed | tf_op | source)
XLA Modules:
  0.0 27.0 jit_solution(17737480791812686446)
XLA Ops:
  0.0 25.4 %shard_map.73 = f32[256,128]{1,0:T(8,128)} custom-call(s32[1,2]{1,0:T(1,128)} %bitcast.11, s32[1,256]{1,0:T(1,128)} %cols_ref.1, s32[1,256]{1,0:T(1,128)} %counts_ref.1, f32[7,1,256]{2,1,0:T(1,128)} %bitcast.10, f32[256,128]{1,0:T(8,128)} %bitcast.8, f32[384,128]{1,0:T(8,128)} %bitcast.7, f32[128,128]{1,0:T(8,128)} %bitcast.9), custom_call_target="tpu_custom_call" | custom-call | tf_op jit(solution)/shard_map/pallas_call | solution.py:452
  25.4 1.6 %copy.9 = f32[4,8,8,128]{3,2,1,0:T(8,128)} copy(f32[4,8,8,128]{3,2,1,0:T(8,128)} %bitcast.6) | data formatting | bytes 262144

commit v4 on v3

--- a/solution.py
+++ b/solution.py
@@ -10,6 +10,7 @@
 FIELDS = 4
 HALO = 3
 SUBSTEPS = 3
+WINDOW = 2
 LEAD = 2
 
 
@@ -44,11 +45,12 @@
 
 def kernel(
     dims,
-    owner_ref, cols_ref, counts_ref, rate_ref, tracer_hbm, flux_hbm, mass_hbm,
-    out_ref,
+    owner_hbm, cols_hbm, counts_hbm, rate_hbm, tracer_hbm, flux_hbm, mass_hbm,
+    out_hbm,
+    owner_ref, cols_ref, counts_ref, rate_ref, out_ref,
     own, inbox, relay, met, state, mid, swept, shapes, halo_out, halo_in, rim_out, rim_in,
     cx, cy, cz, inverse_t, inverse_o, lift,
-    own_sem, state_sem, chain_send, chain_recv, halo_send, halo_recv, rim_send, rim_recv,
+    own_sem, state_sem, small_sem, out_sem, chain_send, chain_recv, halo_send, halo_recv, rim_send, rim_recv,
 ):
     tiles, groups, steps, tracers, levels, cells, lats = dims
     rows = levels * cells
@@ -76,6 +78,13 @@
             own_sem.at[2 * s + 1]))
     for load in loads:
         load.start()
+    smalls = [
+        pltpu.make_async_copy(source, target, small_sem.at[i])
+        for i, (source, target) in enumerate((
+            (owner_hbm, owner_ref), (cols_hbm, cols_ref), (counts_hbm, counts_ref), (rate_hbm, rate_ref)))
+    ]
+    for small in smalls:
+        small.start()
 
     barrier = pltpu.get_barrier_semaphore()
     for neighbour in (left, right):
@@ -132,14 +141,21 @@
             send_sem=chain_send.at[way, c], recv_sem=chain_recv.at[way, c],
             device_id={"trc": to}, device_id_type=pl.DeviceIdType.MESH)
 
-    @pl.when(at_end)
-    def _():
-        for c in range(chunk_total):
-            chain_copy(c, near, near_to, raw(c)).start()
+    def pump(start, stop):
+        @pl.when(at_end)
+        def _():
+            for c in range(start, stop):
+                if c >= WINDOW:
+                    chain_copy(c - WINDOW, near, near_to, raw(c - WINDOW)).wait_send()
+                chain_copy(c, near, near_to, raw(c)).start()
+
+    pump(0, min(WINDOW, chunk_total))
 
     for side in (0, 1):
         halo_copy(0, side, 0, tracers).start()
 
+    for small in smalls:
+        small.wait()
     cols = cols_ref[...]
     x_start = jnp.zeros_like(cols)
     for x in range(1, cells):
@@ -361,11 +377,18 @@
     def sweep_xs(s):
         each_group(lambda p, some: [sweep_x(s, t) for t in some])
 
+    def out_copy(t):
+        at = block(t, rows)
+        return pltpu.make_async_copy(out_ref.at[at], out_hbm.at[at], out_sem.at[t])
+
     def sweep_zs(s):
         def run(p, some):
             for t in some:
                 sweep_z(s, t)
-            if s < steps - 1:
+            if s == steps - 1:
+                for t in some:
+                    out_copy(t).start()
+            else:
                 for t in some:
                     pack_halo(s + 1, t, state, pl.multiple_of(t * rows, rows))
                     for side in (0, 1):
@@ -388,7 +411,9 @@
     for side in (0, 1):
         halo_copy(0, side, 0, tracers).wait_recv()
     near_if(0)
+    pump(WINDOW, min(WINDOW + 2, chunk_total))
     shape_xs(0)
+    pump(WINDOW + 2, chunk_total)
     for c in range(1, LEAD):
         near_if(c)
     links(0, FIELDS - (steps == 1))
@@ -432,13 +457,18 @@
         for t in range(tracers):
             for side in (0, 1):
                 halo_copy(s, side, t, 1).wait_send()
-    for c in range(chunk_total):
+    for c in range(max(chunk_total - WINDOW, 0), chunk_total):
         chain_copy(c, near, near_to).wait_send()
 
     @pl.when(inner)
     def _():
         for c in range(chunk_total):
+            if c < chunk_total - WINDOW:
+                chain_copy(c, near, near_to).wait_send()
             chain_copy(c, far, far_to).wait_send()
+
+    for t in range(tracers):
+        out_copy(t).wait()
 
 
 def body(dims, tracers, flux_pool, mass_pool, owner, conv_cols, conv_steps, conv_rate):
@@ -446,15 +476,19 @@
     rows = levels * cells
     total = steps * FIELDS
     flat = (count * rows, lats)
-    vmem = pl.BlockSpec(memory_space=pltpu.VMEM)
     hbm = pl.BlockSpec(memory_space=pl.ANY)
     f32 = jnp.float32
     out = pl.pallas_call(
         functools.partial(kernel, dims),
         out_shape=jax.ShapeDtypeStruct(flat, f32),
-        in_specs=[pl.BlockSpec(memory_space=pltpu.SMEM), vmem, vmem, vmem, hbm, hbm, hbm],
-        out_specs=vmem,
+        in_specs=[hbm] * 7,
+        out_specs=hbm,
         scratch_shapes=[
+            pltpu.SMEM((1, steps), jnp.int32),
+            pltpu.VMEM(conv_cols.shape, jnp.int32),
+            pltpu.VMEM(conv_steps.shape, jnp.int32),
+            pltpu.VMEM((levels - 1, 1, conv_cols.shape[1]), f32),
+            pltpu.VMEM(flat, f32),
             pltpu.VMEM((total * rows, lats), f32),
             pltpu.VMEM((2, total * rows, lats), f32),
             pltpu.VMEM((2, total * rows, lats), f32),
@@ -475,6 +509,8 @@
             pltpu.VMEM((SUBSTEPS * (levels - 1) * cells, lats), f32),
             pltpu.SemaphoreType.DMA((2 * steps,)),
             pltpu.SemaphoreType.DMA,
+            pltpu.SemaphoreType.DMA((4,)),
+            pltpu.SemaphoreType.DMA((count,)),
             pltpu.SemaphoreType.DMA((2, total)),
             pltpu.SemaphoreType.DMA((2, total)),
             pltpu.SemaphoreType.DMA((steps, 2, count)),

time: 27.2 us -> 26.1 us (0.960)
  the two profiles are of different devices: /device:TPU:0 before, /device:TPU:3 now
where the time goes in v4:
time: 26.1 us; the launch traced here: 25.9 us
  Pallas kernels  24.4 us (93%)
  local copies, waits for them, and re-layouts  1.57 us (6%)
    pallas_call x1, Pallas kernels, body(): pl.pallas_call(functools.partial(kernel, dims), out_shape=jax.ShapeDtypeS...  24.4 us
    unnamed x1, local copies, waits for them, and re-layouts  1.57 us

profile of v4, /device:TPU:3, one launch (start us, length us, event | category | flops | bytes accessed | tf_op | source)
XLA Modules:
  0.0 25.9 jit_solution(15678812596343625212)
XLA Ops:
  0.0 24.4 %shard_map.73 = f32[256,128]{1,0:T(8,128)} custom-call(s32[1,2]{1,0:T(1,128)} %bitcast.11, s32[1,256]{1,0:T(1,128)} %cols_hbm.1, s32[1,256]{1,0:T(1,128)} %counts_hbm.1, f32[7,1,256]{2,1,0:T(1,128)} %bitcast.10, f32[256,128]{1,0:T(8,128)} %bitcast.8, f32[384,128]{1,0:T(8,128)} %bitcast.7, f32[128,128]{1,0:T(8,128)} %bitcast.9), custom_call_target="tpu_custom_call" | custom-call | tf_op jit(solution)/shard_map/pallas_call | solution.py:481
  24.4 1.6 %copy.9 = f32[4,8,8,128]{3,2,1,0:T(8,128)} copy(f32[4,8,8,128]{3,2,1,0:T(8,128)} %bitcast.6) | data formatting | bytes 262144

commit v5 on v4

--- a/solution.py
+++ b/solution.py
@@ -10,8 +10,9 @@
 FIELDS = 4
 HALO = 3
 SUBSTEPS = 3
-WINDOW = 2
-LEAD = 2
+SPLIT = 2
+WINDOW = 4
+LEAD = 3 * SPLIT
 
 
 def face_terms(flux, left_inverse, right_inverse):
@@ -64,7 +65,9 @@
     far_to = me - 1 + 2 * near
     at_end = jnp.logical_or(me == 0, me == groups - 1)
     inner = jnp.logical_and(me > 0, me < groups - 1)
-    chunk_total = steps * FIELDS
+    split = SPLIT if levels % SPLIT == 0 else 1
+    part = rows // split
+    chunk_total = steps * FIELDS * split
 
     load_state = pltpu.make_async_copy(tracer_hbm, state, state_sem)
     load_state.start()
@@ -126,13 +129,14 @@
     pl.semaphore_wait(barrier, expected)
 
     def raw(c):
-        s, field = divmod(c, FIELDS)
+        s, field = divmod(c // split, FIELDS)
+        start = c % split * part
         if field == 0:
-            return mass_hbm.at[pl.ds(s * rows, rows)]
-        return flux_hbm.at[pl.ds((s * 3 + field - 1) * rows, rows)]
+            return mass_hbm.at[pl.ds(s * rows + start, part)]
+        return flux_hbm.at[pl.ds((s * 3 + field - 1) * rows + start, part)]
 
     def chunk(c):
-        return pl.ds(c * rows, rows) if isinstance(c, int) else block(c, rows)
+        return pl.ds(c * part, part)
 
     def chain_copy(c, way, to, source=None):
         at = chunk(c)
@@ -179,7 +183,7 @@
         load.wait()
 
     def owner_of(s):
-        return jnp.full((rows, lats), owner_ref[0, s], jnp.int32)
+        return jnp.full((part, lats), owner_ref[0, s], jnp.int32)
 
     def pass_on(s, c, way, to):
         at = chunk(c)
@@ -369,7 +373,7 @@
 
     def near_if(c):
         if c < chunk_total:
-            near_step(c // FIELDS, c)
+            near_step(c // (FIELDS * split), c)
 
     def shape_xs(s):
         each_group(lambda p, some: [shape_x(s, t) for t in some])
@@ -395,18 +399,19 @@
                         halo_copy(s + 1, side, t, 1).start()
         each_group(run)
 
-    def link(c):
-        s, field = divmod(c, FIELDS)
-        near_if(c + LEAD)
-        far_step(s, c)
+    def link(f):
+        s, field = divmod(f, FIELDS)
+        for c in range(f * split, (f + 1) * split):
+            near_if(c + LEAD)
+            far_step(s, c)
         if field == 0 and s == 0:
             mass_terms(s)
         if field == 1:
             start_rim(s)
 
     def links(start, stop):
-        for c in range(start, min(stop, chunk_total)):
-            link(c)
+        for f in range(start, min(stop, steps * FIELDS)):
+            link(f)
 
     for side in (0, 1):
         halo_copy(0, side, 0, tracers).wait_recv()
@@ -419,7 +424,7 @@
     links(0, FIELDS - (steps == 1))
     for s in range(steps):
         follow = (s + 1) * FIELDS
-        last = chunk_total - 1
+        last = range(chunk_total - split, chunk_total)
         final = s == steps - 1
         if s > 0:
             links(follow - 2, follow - final)
@@ -427,7 +432,8 @@
         if final:
             @pl.when(inner)
             def _():
-                far_arrives(s, last)
+                for c in last:
+                    far_arrives(s, c)
         if s > 0:
             each_group(lambda p, some: halo_arrives(s, some))
             shape_xs(s)
@@ -439,9 +445,11 @@
         if final:
             @pl.when(at_end)
             def _():
-                far_arrives(s, last)
-
-            choose(s, last)
+                for c in last:
+                    far_arrives(s, c)
+
+            for c in last:
+                choose(s, c)
         else:
             links(follow, follow + 1)
         z_terms(s)
@@ -475,6 +483,7 @@
     _, _, steps, count, levels, cells, lats = dims
     rows = levels * cells
     total = steps * FIELDS
+    chunks = total * SPLIT
     flat = (count * rows, lats)
     hbm = pl.BlockSpec(memory_space=pl.ANY)
     f32 = jnp.float32
@@ -511,8 +520,8 @@
             pltpu.SemaphoreType.DMA,
             pltpu.SemaphoreType.DMA((4,)),
             pltpu.SemaphoreType.DMA((count,)),
-            pltpu.SemaphoreType.DMA((2, total)),
-            pltpu.SemaphoreType.DMA((2, total)),
+            pltpu.SemaphoreType.DMA((2, chunks)),
+            pltpu.SemaphoreType.DMA((2, chunks)),
             pltpu.SemaphoreType.DMA((steps, 2, count)),
             pltpu.SemaphoreType.DMA((steps, 2, count)),
             pltpu.SemaphoreType.DMA((steps, 2)),

time: 26.1 us -> 25.9 us (level)
  the two profiles are of different devices: /device:TPU:3 before, /device:TPU:0 now
where the time goes in v5:
time: 25.9 us; the launch traced here: 25.8 us
  Pallas kernels  24.2 us (93%)
  local copies, waits for them, and re-layouts  1.57 us (6%)
    pallas_call x1, Pallas kernels, body(): pl.pallas_call(functools.partial(kernel, dims), out_shape=jax.ShapeDtypeS...  24.2 us
    unnamed x1, local copies, waits for them, and re-layouts  1.57 us

profile of v5, /device:TPU:0, one launch (start us, length us, event | category | flops | bytes accessed | tf_op | source)
XLA Modules:
  0.0 25.8 jit_solution(10898558508542165656)
XLA Ops:
  0.0 24.2 %shard_map.73 = f32[256,128]{1,0:T(8,128)} custom-call(s32[1,2]{1,0:T(1,128)} %bitcast.11, s32[1,256]{1,0:T(1,128)} %cols_hbm.1, s32[1,256]{1,0:T(1,128)} %counts_hbm.1, f32[7,1,256]{2,1,0:T(1,128)} %bitcast.10, f32[256,128]{1,0:T(8,128)} %bitcast.8, f32[384,128]{1,0:T(8,128)} %bitcast.7, f32[128,128]{1,0:T(8,128)} %bitcast.9), custom_call_target="tpu_custom_call" | custom-call | tf_op jit(solution)/shard_map/pallas_call | solution.py:490
  24.2 1.6 %copy.9 = f32[4,8,8,128]{3,2,1,0:T(8,128)} copy(f32[4,8,8,128]{3,2,1,0:T(8,128)} %bitcast.6) | data formatting | bytes 262144

commit v6 on v5

--- a/solution.py
+++ b/solution.py
@@ -10,8 +10,7 @@
 FIELDS = 4
 HALO = 3
 SUBSTEPS = 3
-SPLIT = 2
-WINDOW = 4
+SPLIT = 1
 LEAD = 3 * SPLIT
 
 
@@ -69,6 +68,18 @@
     part = rows // split
     chunk_total = steps * FIELDS * split
 
+    barrier = pltpu.get_barrier_semaphore()
+    for neighbour in (left, right):
+        pl.semaphore_signal(barrier, inc=1, device_id={"tile": neighbour}, device_id_type=pl.DeviceIdType.MESH)
+
+    @pl.when(me > 0)
+    def _():
+        pl.semaphore_signal(barrier, inc=1, device_id={"trc": me - 1}, device_id_type=pl.DeviceIdType.MESH)
+
+    @pl.when(me < groups - 1)
+    def _():
+        pl.semaphore_signal(barrier, inc=1, device_id={"trc": me + 1}, device_id_type=pl.DeviceIdType.MESH)
+
     load_state = pltpu.make_async_copy(tracer_hbm, state, state_sem)
     load_state.start()
     loads = []
@@ -89,18 +100,6 @@
     for small in smalls:
         small.start()
 
-    barrier = pltpu.get_barrier_semaphore()
-    for neighbour in (left, right):
-        pl.semaphore_signal(barrier, inc=1, device_id={"tile": neighbour}, device_id_type=pl.DeviceIdType.MESH)
-
-    @pl.when(me > 0)
-    def _():
-        pl.semaphore_signal(barrier, inc=1, device_id={"trc": me - 1}, device_id_type=pl.DeviceIdType.MESH)
-
-    @pl.when(me < groups - 1)
-    def _():
-        pl.semaphore_signal(barrier, inc=1, device_id={"trc": me + 1}, device_id_type=pl.DeviceIdType.MESH)
-
     def cell_rows(base, x):
         return pl.ds(base + x, levels, stride=cells)
 
@@ -121,10 +120,6 @@
             send_sem=halo_send.at[s, side, t], recv_sem=halo_recv.at[s, side, t],
             device_id={"tile": left if side else right}, device_id_type=pl.DeviceIdType.MESH)
 
-    load_state.wait()
-    for t in range(tracers):
-        pack_halo(0, t, state, t * rows)
-
     expected = 2 + jnp.where(me > 0, 1, 0) + jnp.where(me < groups - 1, 1, 0)
     pl.semaphore_wait(barrier, expected)
 
@@ -145,16 +140,14 @@
             send_sem=chain_send.at[way, c], recv_sem=chain_recv.at[way, c],
             device_id={"trc": to}, device_id_type=pl.DeviceIdType.MESH)
 
-    def pump(start, stop):
-        @pl.when(at_end)
-        def _():
-            for c in range(start, stop):
-                if c >= WINDOW:
-                    chain_copy(c - WINDOW, near, near_to, raw(c - WINDOW)).wait_send()
-                chain_copy(c, near, near_to, raw(c)).start()
-
-    pump(0, min(WINDOW, chunk_total))
-
+    @pl.when(at_end)
+    def _():
+        for c in range(chunk_total):
+            chain_copy(c, near, near_to, raw(c)).start()
+
+    load_state.wait()
+    for t in range(tracers):
+        pack_halo(0, t, state, t * rows)
     for side in (0, 1):
         halo_copy(0, side, 0, tracers).start()
 
@@ -416,9 +409,7 @@
     for side in (0, 1):
         halo_copy(0, side, 0, tracers).wait_recv()
     near_if(0)
-    pump(WINDOW, min(WINDOW + 2, chunk_total))
     shape_xs(0)
-    pump(WINDOW + 2, chunk_total)
     for c in range(1, LEAD):
         near_if(c)
     links(0, FIELDS - (steps == 1))
@@ -465,14 +456,12 @@
         for t in range(tracers):
             for side in (0, 1):
                 halo_copy(s, side, t, 1).wait_send()
-    for c in range(max(chunk_total - WINDOW, 0), chunk_total):
+    for c in range(chunk_total):
         chain_copy(c, near, near_to).wait_send()
 
     @pl.when(inner)
     def _():
         for c in range(chunk_total):
-            if c < chunk_total - WINDOW:
-                chain_copy(c, near, near_to).wait_send()
             chain_copy(c, far, far_to).wait_send()
 
     for t in range(tracers):
@@ -491,7 +480,7 @@
         functools.partial(kernel, dims),
         out_shape=jax.ShapeDtypeStruct(flat, f32),
         in_specs=[hbm] * 7,
-        out_specs=hbm,
+        out_specs=pl.BlockSpec(memory_space=pl.ANY),
         scratch_shapes=[
             pltpu.SMEM((1, steps), jnp.int32),
             pltpu.VMEM(conv_cols.shape, jnp.int32),

time: 25.9 us -> 26.4 us (1.019)
  Pallas kernels: 24.2 us -> 24.7 us
    pallas_call x1, Pallas kernels: 24.2 us -> 24.7 us  [body(): pl.pallas_call(functools.partial(kernel, dims), out_shape=jax.ShapeDtypeS...]
where the time goes in v6:
time: 26.4 us; the launch traced here: 26.2 us
  Pallas kernels  24.7 us (94%)
  local copies, waits for them, and re-layouts  1.57 us (6%)
    pallas_call x1, Pallas kernels, body(): pl.pallas_call(functools.partial(kernel, dims), out_shape=jax.ShapeDtypeS...  24.7 us
    unnamed x1, local copies, waits for them, and re-layouts  1.57 us

profile of v6, /device:TPU:0, one launch (start us, length us, event | category | flops | bytes accessed | tf_op | source)
XLA Modules:
  0.0 26.2 jit_solution(12265536104534175550)
XLA Ops:
  0.0 24.7 %shard_map.73 = f32[256,128]{1,0:T(8,128)} custom-call(s32[1,2]{1,0:T(1,128)} %bitcast.11, s32[1,256]{1,0:T(1,128)} %cols_hbm.1, s32[1,256]{1,0:T(1,128)} %counts_hbm.1, f32[7,1,256]{2,1,0:T(1,128)} %bitcast.10, f32[256,128]{1,0:T(8,128)} %bitcast.8, f32[384,128]{1,0:T(8,128)} %bitcast.7, f32[128,128]{1,0:T(8,128)} %bitcast.9), custom_call_target="tpu_custom_call" | custom-call | tf_op jit(solution)/shard_map/pallas_call | solution.py:479
  24.7 1.6 %copy.9 = f32[4,8,8,128]{3,2,1,0:T(8,128)} copy(f32[4,8,8,128]{3,2,1,0:T(8,128)} %bitcast.6) | data formatting | bytes 262144

commit v7 on v6

--- a/solution.py
+++ b/solution.py
@@ -11,6 +11,7 @@
 HALO = 3
 SUBSTEPS = 3
 SPLIT = 1
+WINDOW = 3
 LEAD = 3 * SPLIT
 
 
@@ -140,17 +141,22 @@
             send_sem=chain_send.at[way, c], recv_sem=chain_recv.at[way, c],
             device_id={"trc": to}, device_id_type=pl.DeviceIdType.MESH)
 
-    @pl.when(at_end)
-    def _():
-        for c in range(chunk_total):
-            chain_copy(c, near, near_to, raw(c)).start()
-
+    def pump(start, stop):
+        @pl.when(at_end)
+        def _():
+            for c in range(min(start, chunk_total), min(stop, chunk_total)):
+                if c >= WINDOW:
+                    chain_copy(c - WINDOW, near, near_to, raw(c - WINDOW)).wait_send()
+                chain_copy(c, near, near_to, raw(c)).start()
+
+    pump(0, WINDOW)
     load_state.wait()
     for t in range(tracers):
         pack_halo(0, t, state, t * rows)
     for side in (0, 1):
         halo_copy(0, side, 0, tracers).start()
 
+    pump(WINDOW, WINDOW + 1)
     for small in smalls:
         small.wait()
     cols = cols_ref[...]
@@ -172,6 +178,7 @@
             lift[pl.ds((n * (levels - 1) + k) * cells, cells), :] = jnp.where(
                 count > n + 0.5, dense[(k + 1) * cells:(k + 2) * cells], 0.0)
 
+    pump(WINDOW + 1, WINDOW + 3)
     for load in loads:
         load.wait()
 
@@ -410,6 +417,7 @@
         halo_copy(0, side, 0, tracers).wait_recv()
     near_if(0)
     shape_xs(0)
+    pump(WINDOW + 3, chunk_total)
     for c in range(1, LEAD):
         near_if(c)
     links(0, FIELDS - (steps == 1))
@@ -456,12 +464,14 @@
         for t in range(tracers):
             for side in (0, 1):
                 halo_copy(s, side, t, 1).wait_send()
-    for c in range(chunk_total):
+    for c in range(max(chunk_total - WINDOW, 0), chunk_total):
         chain_copy(c, near, near_to).wait_send()
 
     @pl.when(inner)
     def _():
         for c in range(chunk_total):
+            if c < chunk_total - WINDOW:
+                chain_copy(c, near, near_to).wait_send()
             chain_copy(c, far, far_to).wait_send()
 
     for t in range(tracers):

time: 26.4 us -> 26.4 us (level)
  no operation moved by 1% of the time
where the time goes in v7:
time: 26.4 us; the launch traced here: 26.3 us
  Pallas kernels  24.7 us (94%)
  local copies, waits for them, and re-layouts  1.57 us (6%)
    pallas_call x1, Pallas kernels, body(): pl.pallas_call(functools.partial(kernel, dims), out_shape=jax.ShapeDtypeS...  24.7 us
    unnamed x1, local copies, waits for them, and re-layouts  1.57 us

profile of v7, /device:TPU:0, one launch (start us, length us, event | category | flops | bytes accessed | tf_op | source)
XLA Modules:
  0.0 26.3 jit_solution(9423892697496900320)
XLA Ops:
  0.0 24.7 %shard_map.73 = f32[256,128]{1,0:T(8,128)} custom-call(s32[1,2]{1,0:T(1,128)} %bitcast.11, s32[1,256]{1,0:T(1,128)} %cols_hbm.1, s32[1,256]{1,0:T(1,128)} %counts_hbm.1, f32[7,1,256]{2,1,0:T(1,128)} %bitcast.10, f32[256,128]{1,0:T(8,128)} %bitcast.8, f32[384,128]{1,0:T(8,128)} %bitcast.7, f32[128,128]{1,0:T(8,128)} %bitcast.9), custom_call_target="tpu_custom_call" | custom-call | tf_op jit(solution)/shard_map/pallas_call | solution.py:489
  24.7 1.6 %copy.9 = f32[4,8,8,128]{3,2,1,0:T(8,128)} copy(f32[4,8,8,128]{3,2,1,0:T(8,128)} %bitcast.6) | data formatting | bytes 262144

commit v8 on v7

--- a/solution.py
+++ b/solution.py
@@ -10,6 +10,7 @@
 FIELDS = 4
 HALO = 3
 SUBSTEPS = 3
+VMEM_BYTES = 16 * 1024 * 1024
 SPLIT = 1
 WINDOW = 3
 LEAD = 3 * SPLIT
@@ -47,11 +48,11 @@
 def kernel(
     dims,
     owner_hbm, cols_hbm, counts_hbm, rate_hbm, tracer_hbm, flux_hbm, mass_hbm,
-    out_hbm,
-    owner_ref, cols_ref, counts_ref, rate_ref, out_ref,
+    out_ref,
+    owner_ref, cols_ref, counts_ref, rate_ref,
     own, inbox, relay, met, state, mid, swept, shapes, halo_out, halo_in, rim_out, rim_in,
     cx, cy, cz, inverse_t, inverse_o, lift,
-    own_sem, state_sem, small_sem, out_sem, chain_send, chain_recv, halo_send, halo_recv, rim_send, rim_recv,
+    own_sem, state_sem, small_sem, chain_send, chain_recv, halo_send, halo_recv, rim_send, rim_recv,
 ):
     tiles, groups, steps, tracers, levels, cells, lats = dims
     rows = levels * cells
@@ -381,18 +382,11 @@
     def sweep_xs(s):
         each_group(lambda p, some: [sweep_x(s, t) for t in some])
 
-    def out_copy(t):
-        at = block(t, rows)
-        return pltpu.make_async_copy(out_ref.at[at], out_hbm.at[at], out_sem.at[t])
-
     def sweep_zs(s):
         def run(p, some):
             for t in some:
                 sweep_z(s, t)
-            if s == steps - 1:
-                for t in some:
-                    out_copy(t).start()
-            else:
+            if s < steps - 1:
                 for t in some:
                     pack_halo(s + 1, t, state, pl.multiple_of(t * rows, rows))
                     for side in (0, 1):
@@ -474,9 +468,6 @@
                 chain_copy(c, near, near_to).wait_send()
             chain_copy(c, far, far_to).wait_send()
 
-    for t in range(tracers):
-        out_copy(t).wait()
-
 
 def body(dims, tracers, flux_pool, mass_pool, owner, conv_cols, conv_steps, conv_rate):
     _, _, steps, count, levels, cells, lats = dims
@@ -486,17 +477,20 @@
     flat = (count * rows, lats)
     hbm = pl.BlockSpec(memory_space=pl.ANY)
     f32 = jnp.float32
+    operands = (
+        owner.T, conv_cols, conv_steps, jnp.transpose(conv_rate, (1, 0, 2)), tracers.reshape(flat),
+        flux_pool.reshape(steps * 3 * rows, lats), mass_pool.reshape(steps * rows, lats),
+    )
     out = pl.pallas_call(
         functools.partial(kernel, dims),
-        out_shape=jax.ShapeDtypeStruct(flat, f32),
+        out_shape=pltpu.VMEM(flat, f32),
         in_specs=[hbm] * 7,
-        out_specs=pl.BlockSpec(memory_space=pl.ANY),
+        out_specs=pl.BlockSpec(memory_space=pltpu.VMEM),
         scratch_shapes=[
             pltpu.SMEM((1, steps), jnp.int32),
             pltpu.VMEM(conv_cols.shape, jnp.int32),
             pltpu.VMEM(conv_steps.shape, jnp.int32),
             pltpu.VMEM((levels - 1, 1, conv_cols.shape[1]), f32),
-            pltpu.VMEM(flat, f32),
             pltpu.VMEM((total * rows, lats), f32),
             pltpu.VMEM((2, total * rows, lats), f32),
             pltpu.VMEM((2, total * rows, lats), f32),
@@ -518,7 +512,6 @@
             pltpu.SemaphoreType.DMA((2 * steps,)),
             pltpu.SemaphoreType.DMA,
             pltpu.SemaphoreType.DMA((4,)),
-            pltpu.SemaphoreType.DMA((count,)),
             pltpu.SemaphoreType.DMA((2, chunks)),
             pltpu.SemaphoreType.DMA((2, chunks)),
             pltpu.SemaphoreType.DMA((steps, 2, count)),
@@ -526,11 +519,8 @@
             pltpu.SemaphoreType.DMA((steps, 2)),
             pltpu.SemaphoreType.DMA((steps, 2)),
         ],
-        compiler_params=pltpu.CompilerParams(collective_id=0, has_side_effects=True),
-    )(
-        owner.T, conv_cols, conv_steps, jnp.transpose(conv_rate, (1, 0, 2)), tracers.reshape(flat),
-        flux_pool.reshape(steps * 3 * rows, lats), mass_pool.reshape(steps * rows, lats),
-    )
+        compiler_params=pltpu.CompilerParams(collective_id=0, has_side_effects=True, vmem_limit_bytes=VMEM_BYTES),
+    )(*(pltpu.with_memory_space_constraint(x, pltpu.HBM) for x in operands))
     return out.reshape(tracers.shape)
 
 

time: 26.4 us -> 24.9 us (0.943)
  local copies, waits for them, and re-layouts: 1.57 us -> 0.66 us
  Pallas kernels: 24.7 us -> 24.1 us
    unnamed x1, local copies, waits for them, and re-layouts: 1.57 us -> 0.66 us
    pallas_call x1, Pallas kernels: 24.7 us -> 24.1 us  [body(): pl.pallas_call(functools.partial(kernel, dims), out_shape=pltpu.VMEM(flat...]
where the time goes in v8:
time: 24.9 us; the launch traced here: 24.7 us
  Pallas kernels  24.1 us (97%)
  local copies, waits for them, and re-layouts  0.66 us (3%)
    pallas_call x1, Pallas kernels, body(): pl.pallas_call(functools.partial(kernel, dims), out_shape=pltpu.VMEM(flat...  24.1 us
    unnamed x1, local copies, waits for them, and re-layouts  0.66 us

profile of v8, /device:TPU:0, one launch (start us, length us, event | category | flops | bytes accessed | tf_op | source)
XLA Modules:
  0.0 24.7 jit_solution(6256414706000068943)
XLA Ops:
  0.0 24.1 %shard_map.73 = f32[256,128]{1,0:T(8,128)S(1)} custom-call(s32[1,2]{1,0:T(1,128)} %bitcast.11, s32[1,256]{1,0:T(1,128)} %cols_hbm.1, s32[1,256]{1,0:T(1,128)} %counts_hbm.1, f32[7,1,256]{2,1,0:T(1,128)} %bitcast.10, f32[256,128]{1,0:T(8,128)} %bitcast.8, f32[384,128]{1,0:T(8,128)} %bitcast.7, f32[128,128]{1,0:T(8,128)} %bitcast.9), custom_call_target="tpu_custom_call" | custom-call | tf_op jit(solution)/shard_map/pallas_call | solution.py:484
  24.1 0.7 %copy.9 = f32[4,8,8,128]{3,2,1,0:T(8,128)} copy(f32[4,8,8,128]{3,2,1,0:T(8,128)S(1)} %bitcast.6) | data formatting | bytes 262144

commit v9 on v8

--- a/solution.py
+++ b/solution.py
@@ -11,8 +11,8 @@
 HALO = 3
 SUBSTEPS = 3
 VMEM_BYTES = 16 * 1024 * 1024
-SPLIT = 1
-WINDOW = 3
+SPLIT = 2
+WINDOW = 64
 LEAD = 3 * SPLIT
 
 

time: 24.9 us -> 24.9 us (level)
  no operation moved by 1% of the time
where the time goes in v9:
time: 24.9 us; the launch traced here: 24.8 us
  Pallas kernels  24.1 us (97%)
  local copies, waits for them, and re-layouts  0.66 us (3%)
    pallas_call x1, Pallas kernels, body(): pl.pallas_call(functools.partial(kernel, dims), out_shape=pltpu.VMEM(flat...  24.1 us
    unnamed x1, local copies, waits for them, and re-layouts  0.66 us

profile of v9, /device:TPU:0, one launch (start us, length us, event | category | flops | bytes accessed | tf_op | source)
XLA Modules:
  0.0 24.8 jit_solution(14111997989346648737)
XLA Ops:
  0.0 24.1 %shard_map.73 = f32[256,128]{1,0:T(8,128)S(1)} custom-call(s32[1,2]{1,0:T(1,128)} %bitcast.11, s32[1,256]{1,0:T(1,128)} %cols_hbm.1, s32[1,256]{1,0:T(1,128)} %counts_hbm.1, f32[7,1,256]{2,1,0:T(1,128)} %bitcast.10, f32[256,128]{1,0:T(8,128)} %bitcast.8, f32[384,128]{1,0:T(8,128)} %bitcast.7, f32[128,128]{1,0:T(8,128)} %bitcast.9), custom_call_target="tpu_custom_call" | custom-call | tf_op jit(solution)/shard_map/pallas_call | solution.py:484
  24.1 0.7 %copy.9 = f32[4,8,8,128]{3,2,1,0:T(8,128)} copy(f32[4,8,8,128]{3,2,1,0:T(8,128)S(1)} %bitcast.6) | data formatting | bytes 262144

commit v10 on v8

--- a/solution.py
+++ b/solution.py
@@ -354,7 +354,7 @@
         for k in range(levels):
             target[pl.ds(base + k * cells, cells), :] = q[k]
 
-    together = 2 if tracers % 2 == 0 else 1
+    together = next(n for n in (4, 2, 1) if tracers % n == 0)
     loops = tracers // together
 
     def each_group(body):

time: 24.9 us -> 23.9 us (0.960)
  Pallas kernels: 24.1 us -> 23 us
    pallas_call x1, Pallas kernels: 24.1 us -> 23 us  [body(): pl.pallas_call(functools.partial(kernel, dims), out_shape=pltpu.VMEM(flat...]
where the time goes in v10:
time: 23.9 us; the launch traced here: 23.7 us
  Pallas kernels  23 us (96%)
  local copies, waits for them, and re-layouts  0.66 us (3%)
    pallas_call x1, Pallas kernels, body(): pl.pallas_call(functools.partial(kernel, dims), out_shape=pltpu.VMEM(flat...  23 us
    unnamed x1, local copies, waits for them, and re-layouts  0.66 us

profile of v10, /device:TPU:0, one launch (start us, length us, event | category | flops | bytes accessed | tf_op | source)
XLA Modules:
  0.0 23.7 jit_solution(7422970585495921690)
XLA Ops:
  0.0 23.0 %shard_map.73 = f32[256,128]{1,0:T(8,128)S(1)} custom-call(s32[1,2]{1,0:T(1,128)} %bitcast.11, s32[1,256]{1,0:T(1,128)} %cols_hbm.1, s32[1,256]{1,0:T(1,128)} %counts_hbm.1, f32[7,1,256]{2,1,0:T(1,128)} %bitcast.10, f32[256,128]{1,0:T(8,128)} %bitcast.8, f32[384,128]{1,0:T(8,128)} %bitcast.7, f32[128,128]{1,0:T(8,128)} %bitcast.9), custom_call_target="tpu_custom_call" | custom-call | tf_op jit(solution)/shard_map/pallas_call | solution.py:484
  23.1 0.7 %copy.9 = f32[4,8,8,128]{3,2,1,0:T(8,128)} copy(f32[4,8,8,128]{3,2,1,0:T(8,128)S(1)} %bitcast.6) | data formatting | bytes 262144
